TPU v7x, 32 devices: a whole 2x2x4 slice. The times are simulated.
32 devices in a mesh: graph: 8 (over z, core), replica: 4 (over y, x).
Axes of the slice: x: 2, y: 2, z: 4, core: 2. Of those that a mesh axis runs over, the one named last changes fastest.
Arguments:
- features: bfloat16 [4, 1024, 512], P('replica', 'graph'), may hold values from -8 to 8
- neighbours: int32 [4, 1024, 16], P('replica', 'graph'), may hold values from 0 to 143
- send_rows: int32 [4, 8, 8, 2], P('replica', 'graph'), may hold values from 0 to 127
- send_counts: int32 [4, 8, 8], P('replica', 'graph'), may hold values from 0 to 2, as said below
- candidates: int32 [4, 256, 512], P('replica', 'graph'), may hold values from 0 to 127
- perturbation: float32 [4, 256, 4, 512], P('replica', 'graph'), may hold values from -320 to 320
- weight: bfloat16 [512, 512], replicated, may hold values from -0.25 to 0.25
Outputs:
- d_features: bfloat16 [4, 1024, 512], P('replica', 'graph')
- weight_grad: float32 [512, 512], P('graph', 'replica')
Inputs may be any that keep to these rules, and one draw needn't show every extreme that they name: `send_counts`: rows that one device sends to another in its mini-batch; in every draw one device of each mini-batch receives 2 rows from every device.
All inputs are finite; a program needn't handle non-finite values.
Results may differ from a plain program's by a relative error of at most 0.013.
Values may be sent and summed in bfloat16 or wider, within the bound.
No kernel may reach another device: no remote copies, remote signals or barrier semaphores. Data moves between devices by JAX's collectives and lax.ppermute only.
A program may use at most 64 MiB of HBM per device.

v0:
```python
import math

import jax
import jax.numpy as jnp
from jax import lax
from jax.sharding import PartitionSpec as P

TOP = 20


SCORE_SCALE = 16.0
LOSS_SCALE = 16.0
EPSILON = 1e-05


def embed_backward(mean_rows, weight, candidates, perturbation):
    query_count = candidates.shape[0]
    pre = jnp.dot(mean_rows, weight, preferred_element_type=jnp.float32)
    inverse = lax.rsqrt(jnp.mean(pre * pre, axis=-1, keepdims=True) + EPSILON)
    embedded = (pre * inverse).astype(jnp.bfloat16)
    similar = jnp.dot(embedded[:query_count], embedded.T, preferred_element_type=jnp.float32)
    factor = SCORE_SCALE / pre.shape[1]
    scores = factor * jnp.take_along_axis(similar, candidates, axis=1)
    perturbed = scores[:, None, :] + perturbation
    highest = jnp.max(perturbed, axis=-1, keepdims=True)
    exponent = jnp.exp(perturbed - highest)
    weights_soft = exponent / jnp.sum(exponent, axis=-1, keepdims=True)
    target = (jnp.arange(candidates.shape[1], dtype=jnp.int32) < TOP).astype(jnp.float32)
    d_scores = LOSS_SCALE * (TOP * jnp.mean(weights_soft, axis=1) - target[None, :])
    query_index = jnp.broadcast_to(
        jnp.arange(query_count, dtype=jnp.int32)[:, None], candidates.shape
    )
    d_similar = (
        jnp.zeros((query_count, embedded.shape[0]), jnp.float32)
        .at[query_index, candidates]
        .add(d_scores)
        .astype(jnp.bfloat16)
    )
    d_embedded = factor * lax.dot_general(
        d_similar,
        embedded[:query_count],
        (((0,), (0,)), ((), ())),
        preferred_element_type=jnp.float32,
    )
    d_queries = factor * jnp.dot(d_similar, embedded, preferred_element_type=jnp.float32)
    d_embedded = d_embedded.at[:query_count].add(d_queries)
    d_pre = inverse * d_embedded - inverse * inverse * inverse * pre * jnp.mean(
        d_embedded * pre, axis=-1, keepdims=True
    )
    return d_pre.astype(jnp.bfloat16)


def body(features, neighbours, send_rows, send_counts, candidates, perturbation, weight):
    feature_rows = features[0]
    neighbour_rows = neighbours[0]
    outgoing_rows = send_rows[0, 0]
    arriving_counts = send_counts[0, 0]
    groups = lax.axis_size("graph")
    capacity = outgoing_rows.shape[1]
    row_count = feature_rows.shape[0]
    feature_width = feature_rows.shape[1]
    fanout = neighbour_rows.shape[1]
    table_rows = row_count + groups * capacity
    outgoing = feature_rows[outgoing_rows.reshape(-1)].reshape(groups, capacity, feature_width)
    arrived = lax.all_to_all(outgoing, "graph", split_axis=0, concat_axis=0, tiled=True)
    keep = jnp.arange(capacity, dtype=jnp.int32)[None, :] < arriving_counts[:, None]
    halo = jnp.where(keep[:, :, None], arrived, jnp.zeros((), jnp.bfloat16)).reshape(
        groups * capacity, feature_width
    )
    table_index = jnp.arange(table_rows, dtype=jnp.int32)
    counted = jnp.zeros((row_count, table_rows), jnp.float32)
    for column in range(fanout):
        counted = counted + (neighbour_rows[:, column][:, None] == table_index[None, :]).astype(
            jnp.float32
        )
    adjacency = counted.astype(jnp.bfloat16)
    start_total = feature_rows.astype(jnp.float32)
    table = jnp.concatenate([feature_rows, halo], axis=0)
    total = start_total + jnp.dot(adjacency, table, preferred_element_type=jnp.float32)
    mean_rows = (total / (fanout + 1)).astype(jnp.bfloat16)
    d_pre = embed_backward(mean_rows, weight, candidates[0], perturbation[0])
    rows_summed = lax.psum_scatter(
        lax.dot_general(
            mean_rows, d_pre, (((0,), (0,)), ((), ())), preferred_element_type=jnp.float32
        ),
        "graph",
        scatter_dimension=0,
        tiled=True,
    )
    weight_tile = lax.psum_scatter(rows_summed, "replica", scatter_dimension=1, tiled=True)
    weight_grad = weight_tile / math.sqrt(groups * lax.axis_size("replica"))
    share = (
        lax.dot_general(d_pre, weight, (((1,), (1,)), ((), ())), preferred_element_type=jnp.float32)
        / (fanout + 1)
    ).astype(jnp.bfloat16)
    d_table = lax.dot_general(
        adjacency, share, (((0,), (0,)), ((), ())), preferred_element_type=jnp.float32
    )
    d_local = share.astype(jnp.float32) + d_table[:row_count]
    halo_grad = jnp.where(keep.reshape(-1)[:, None], d_table[row_count:], 0.0).astype(jnp.bfloat16)
    returned = lax.all_to_all(
        halo_grad.reshape(groups, capacity, feature_width),
        "graph",
        split_axis=0,
        concat_axis=0,
        tiled=True,
    )
    d_rows = d_local.at[outgoing_rows.reshape(-1)].add(
        returned.reshape(groups * capacity, feature_width).astype(jnp.float32)
    )
    return (d_rows.astype(jnp.bfloat16)[None], weight_grad)


def solution(mesh):
    placed = (
        P("replica", "graph", None),
        P("replica", "graph", None),
        P("replica", "graph", None, None),
        P("replica", "graph", None),
        P("replica", "graph", None),
        P("replica", "graph", None, None),
        P(),
    )
    return jax.shard_map(
        body,
        mesh=mesh,
        in_specs=placed,
        out_specs=(P("replica", "graph", None), P("graph", "replica")),
        check_vma=False,
    )
```

profile of v0, /device:TPU:0, one launch (start us, length us, event | category | flops | bytes accessed | tf_op | source)
XLA Modules:
  0.0 305.9 jit_solution(13796368155200729853)
XLA Ops:
  7.2 0.8 copy.10
  8.1 1.5 gather_fusion
  9.6 0.6 reshape.201
  10.3 6.3 %all-to-all-start = ((bf16[8,2,512]{2,1,0:T(2,128)(2,1)}), bf16[8,2,512]{2,1,0:T(2,128)(2,1)S(1)}, u32[]{:S(2)}, u32[]{:S(2)}) async-start(bf16[8,2,512]{2,1,0:T(2,128)(2,1)} %reshape.201), calls=%async_computation | async-start | bytes 32768 | tf_op jit(solution)/shard_map/all_to_all | solution.py:65
  16.6 1.0 slice_bitcast_fusion.15
  17.6 0.7 iota_compare_fusion.16
  18.4 0.9 or_bitcast_fusion
  19.2 0.7 multiply_reduce_fusion.2
  20.0 0.8 and_reduce_fusion
  20.8 1.4 all-to-all-done
  22.4 0.5 fusion.6
  22.8 0.3 multiply_reduce_fusion.1
  23.4 100.8 %gather_fusion.1 = f32[16384]{0:T(1024)S(1)} fusion(f32[32,128]{1,0:T(8,128)S(1)} %fusion.17, s32[16384]{0:T(1024)S(1)} %bitcast.80), kind=kCustom, calls=%fused_computation.1 | custom fusion | bytes 262144 | tf_op jit(solution)/shard_map/jit(take_along_axis)/gather | solution.py:23
  124.4 0.3 fusion.29
  124.8 113.5 %scatter_custom_fusion.1 = f32[4096]{0:T(1024)S(1)} fusion(s32[16384]{0:T(1024)S(1)} %bitcast.83, f32[16384]{0:T(1024)S(1)} %bitcast.84, f32[]{:T(128)} %constant.70.clone.1), kind=kCustom, calls=%fused_computation.65 | custom fusion | flops 16384 | bytes 16388
  238.8 1.3 fusion.30
  240.6 0.6 fusion.28
  241.2 0.6 reshape.203
  241.8 3.7 %all-to-all-start.1 = ((bf16[8,2,512]{2,1,0:T(2,128)(2,1)}), bf16[8,2,512]{2,1,0:T(2,128)(2,1)S(1)}, u32[]{:S(2)}, u32[]{:S(2)}) async-start(bf16[8,2,512]{2,1,0:T(2,128)(2,1)} %reshape.203), calls=%async_computation.1 | async-start | bytes 32768 | tf_op jit(solution)/shard_map/all_to_all | solution.py:101
  245.6 27.6 %reduce-scatter.3.cloned.1.call-done = f32[64,512]{1,0:T(8,128)} async-done(((f32[512,512]{1,0:T(8,128)}), f32[64,512]{1,0:T(8,128)}) %reduce-scatter.3.cloned.1.call-update) | async-done | bytes 131088 | tf_op jit(solution)/shard_map/reduce_scatter | solution.py:82
  273.3 0.8 scatter_fusion
  274.1 0.7 convert_bitcast_fusion
  274.8 22.9 %reduce-scatter.5.cloned.1.call-done = f32[64,128]{1,0:T(8,128)} async-done(((f32[64,512]{1,0:T(8,128)}), f32[64,128]{1,0:T(8,128)}) %reduce-scatter.5.cloned.1.call-update) | async-done | bytes 32784 | tf_op jit(solution)/shard_map/reduce_scatter | solution.py:90
  297.7 1.4 broadcast_multiply_fusion
  (40 shorter events, 1.8 us)
Async XLA Ops:
  7.2 15.7 %copy-start = (bf16[512,512]{1,0:T(8,128)(2,1)S(1)}, bf16[512,512]{1,0:T(8,128)(2,1)}, u32[]{:S(2)}) copy-start(bf16[512,512]{1,0:T(8,128)(2,1)} %param.15) | copy-start | bytes 1572868
  7.2 15.2 %copy-start.2 = (bf16[1,128,512]{2,1,0:T(8,128)(2,1)S(1)}, bf16[1,128,512]{2,1,0:T(8,128)(2,1)}, u32[]{:S(2)}) copy-start(bf16[1,128,512]{2,1,0:T(8,128)(2,1)} %param.9) | copy-start | bytes 393220
  10.3 12.0 %all-to-all-start = ((bf16[8,2,512]{2,1,0:T(2,128)(2,1)}), bf16[8,2,512]{2,1,0:T(2,128)(2,1)S(1)}, u32[]{:S(2)}, u32[]{:S(2)}) async-start(bf16[8,2,512]{2,1,0:T(2,128)(2,1)} %reshape.201), calls=%async_computation | async-start | bytes 32768 | tf_op jit(solution)/shard_map/all_to_all | solution.py:65
  16.6 256.6 %reduce-scatter.3.cloned.1.call-start = ((), (), s32[]{:S(2)}) async-start(), calls=%async_computation.4 | async-start | bytes 1179648 | tf_op jit(solution)/shard_map/reduce_scatter | solution.py:82
  23.4 100.9 %copy-start.1 = (s32[1,32,512]{2,1,0:T(8,128)S(1)}, s32[1,32,512]{2,1,0:T(8,128)}, u32[]{:S(2)}) copy-start(s32[1,32,512]{2,1,0:T(8,128)} %param.13) | copy-start | bytes 196612
  23.4 100.9 %copy-start.3 = (f32[1,32,4,512]{3,2,1,0:T(4,128)S(1)}, f32[1,32,4,512]{3,2,1,0:T(4,128)}, u32[]{:S(2)}) copy-start(f32[1,32,4,512]{3,2,1,0:T(4,128)} %param.14) | copy-start | bytes 786436
  241.8 31.4 %all-to-all-start.1 = ((bf16[8,2,512]{2,1,0:T(2,128)(2,1)}), bf16[8,2,512]{2,1,0:T(2,128)(2,1)S(1)}, u32[]{:S(2)}, u32[]{:S(2)}) async-start(bf16[8,2,512]{2,1,0:T(2,128)(2,1)} %reshape.203), calls=%async_computation.1 | async-start | bytes 32768 | tf_op jit(solution)/shard_map/all_to_all | solution.py:101
  245.5 52.2 %reduce-scatter.5.cloned.1.call-start = ((), (), s32[]{:S(2)}) async-start(), calls=%async_computation.5 | async-start | bytes 163840 | tf_op jit(solution)/shard_map/reduce_scatter | solution.py:90
Sparse Core Ops, SparseCore 0:
  240.3 32.8 reduce-scatter.2
  275.9 21.7 reduce-scatter.4
where the time goes:
time: 306 us
  other arithmetic  120 us (39%)
  local copies, waits for them, and re-layouts  106 us (35%)
  waiting for transfers between devices  52 us (17%)
  between operations  14.3 us (5%)
  starting transfers between devices  10.1 us (3%)
  matrix products  3.45 us (1%)
    unnamed x6, other arithmetic  116 us
    gather x2, local copies, waits for them, and re-layouts, embed_backward(): scores = factor * jnp.take_along_axis(similar, candidates, axis=1)  101 us
    reduce_scatter x1, waiting for transfers between devices, body(): lax.psum_scatter(lax.dot_general(mean_rows, d_pre, (((0,), (0,)), ((), ()...  27.6 us
    reduce_scatter x1, waiting for transfers between devices, body(): lax.psum_scatter(rows_summed, 'replica', scatter_dimension=1, tiled=True)  22.9 us
    all_to_all x1, starting transfers between devices, body(): lax.all_to_all(outgoing, 'graph', split_axis=0, concat_axis=0, tiled=True)  6.33 us
  transfers between devices with their start and end apart: 4, of which 3 were waited for; matrix products, arithmetic and copies ran while one was open for 2% of the time, Pallas kernels for 0%

commit v1 on v0

v1 whole, which is shorter than its diff:
```python
import functools
import math

import jax
import jax.numpy as jnp
from jax import lax
from jax.experimental import pallas as pl
from jax.experimental.pallas import tpu as pltpu
from jax.sharding import PartitionSpec as P

TOP = 20
SCORE_SCALE = 16.0
LOSS_SCALE = 16.0
EPSILON = 1e-05
LANES = 128
DIGIT = 16
F32 = jnp.float32
BF16 = jnp.bfloat16
NN = (((1,), (0,)), ((), ()))
TN = (((0,), (0,)), ((), ()))
NT = (((1,), (1,)), ((), ()))


def dot(a, b, dims):
    return lax.dot_general(a, b, dims, preferred_element_type=F32)


def slot_device(slot, towers):
    core = lax.axis_index("core")
    pair, e = slot // 2, slot % 2
    mixed = jnp.where(pair > 1, 1, 0)
    odd = pair % 2 * mixed
    upper = pair % 2 * (1 - mixed) + lax.bitwise_xor(core, odd) * mixed
    z = lax.bitwise_xor(lax.axis_index("z"), pair // 2 + upper * (towers // 2))
    return 2 * z + lax.bitwise_xor(core, lax.bitwise_xor(odd, jnp.int32(e)))


def kept_slots(towers):
    return [0, 2] + [4 * j + e for j in range(1, towers // 2) for e in range(2)]


def sent_slots(towers):
    return [1, 3] + [4 * j + 2 + e for j in range(1, towers // 2) for e in range(2)]


def slot_tiles(tiles):
    core = lax.axis_index("core")
    pairs = [xor_order(tiles[2 * z : 2 * z + 2], core) for z in range(len(tiles) // 2)]
    same = xor_order([pair[0] for pair in pairs], lax.axis_index("z"))
    other = xor_order([pair[1] for pair in pairs], lax.axis_index("z"))
    half = len(pairs) // 2
    ordered = [same[0], other[0], same[half], other[half]]
    for j in range(1, half):
        first = [xor_order([found[j], found[half + j]], core) for found in (same, other)]
        ordered += [first[0][0], first[1][0], first[1][1], first[0][1]]
    return ordered


def pick(array, slots, size):
    return jnp.concatenate([array[i * size : (i + 1) * size] for i in slots], axis=0)


def fold(rows):
    return jnp.concatenate(
        [rows[:, j : j + LANES] for j in range(0, rows.shape[1], LANES)], axis=0
    )


def unfold(block, parts):
    size = block.shape[0] // parts
    return jnp.concatenate([block[j * size : (j + 1) * size] for j in range(parts)], axis=1)


def near_rows(kept, arrived, size):
    return jnp.concatenate([pick(kept, [1], size), pick(arrived, [1], size)], axis=0)


def far_rows(kept, arrived, j, size):
    return jnp.concatenate([pick(x, [2 * j, 2 * j + 1], size) for x in (kept, arrived)], axis=0)


def slot_rows(kept, arrived, near, far, passed, size):
    rows = [pick(kept, [0], size), pick(arrived, [0], size), near]
    for j, block in enumerate(far):
        rows += [pick(block, [0, 2], size), pick(passed, [2 * j, 2 * j + 1], size)]
    return jnp.concatenate(rows, axis=0)


def xor_order(pieces, me):
    bit = 1
    while bit < len(pieces):
        swap = lax.bitwise_and(me, jnp.int32(bit)) != 0
        pieces = [jnp.where(swap, pieces[i ^ bit], pieces[i]) for i in range(len(pieces))]
        bit *= 2
    return pieces


def start_copies(pairs, sems):
    copies = [pltpu.make_async_copy(a, b, sems.at[i]) for i, (a, b) in enumerate(pairs)]
    for copy in copies:
        copy.start()
    return copies


def outgoing_kernel(
    towers,
    capacity,
    send_hbm,
    counts_hbm,
    features_hbm,
    neighbours_hbm,
    kept_ref,
    sent_ref,
    onehot_ref,
    held_ref,
    features_ref,
    neighbours_ref,
    send_smem,
    counts_smem,
    sems,
):
    copies = start_copies(
        [
            (send_hbm, send_smem),
            (counts_hbm, counts_smem),
            (features_hbm, features_ref),
            (neighbours_hbm, neighbours_ref),
        ],
        sems,
    )
    rows = features_ref.shape[0]
    slots = 2 * towers * capacity
    slot = lax.broadcasted_iota(jnp.int32, (slots, rows), 0)
    row = lax.broadcasted_iota(jnp.int32, (slots, rows), 1)
    named = jnp.full((slots, rows), -1, jnp.int32)
    held = jnp.zeros((slots, rows), jnp.int32)
    copies[0].wait()
    copies[1].wait()
    for i in range(2 * towers):
        device = slot_device(i, towers)
        held = jnp.where(slot // capacity == i, counts_smem[0, device], held)
        for k in range(capacity):
            named = jnp.where(slot == i * capacity + k, send_smem[k, device], named)
    onehot = (named == row).astype(F32).astype(BF16)
    onehot_ref[...] = onehot
    held_ref[...] = (slot % capacity < held).astype(F32)
    copies[2].wait()
    picked = dot(onehot, features_ref[...], NN)
    kept_ref[...] = pick(picked, kept_slots(towers), capacity)
    sent_ref[...] = pick(picked, sent_slots(towers), capacity)
    copies[3].wait()


def hop_kernel(capacity, after_ref, kept_ref, arrived_ref, near_ref, *far_refs):
    kept, arrived = kept_ref[...], arrived_ref[...]
    near_ref[...] = near_rows(kept, arrived, capacity).astype(BF16)
    for j, ref in enumerate(far_refs):
        ref[...] = far_rows(kept, arrived, j + 1, capacity).astype(BF16)


def pass_kernel(capacity, *refs):
    far_refs, out_ref = refs[:-1], refs[-1]
    rows = [pick(ref[...].astype(F32), [1, 3], capacity) for ref in far_refs]
    out_ref[...] = jnp.concatenate(rows, axis=0).astype(BF16)


def adjacency_kernel(
    towers,
    capacity,
    held_ref,
    features_ref,
    neighbours_ref,
    own_ref,
    far_ref,
    far_turned_ref,
    start_ref,
):
    rows = features_ref.shape[0]
    fanout = neighbours_ref.shape[0]
    slots = far_ref.shape[0]
    own = lax.broadcasted_iota(jnp.int32, (rows, rows), 0)
    far = lax.broadcasted_iota(jnp.int32, (slots, rows), 0)
    far_slot = slot_device(far // capacity, towers) * capacity + far % capacity + rows
    own_count = jnp.zeros((rows, rows), F32)
    far_count = jnp.zeros((slots, rows), F32)
    for f in range(fanout):
        named = neighbours_ref[f : f + 1, :]
        own_count = own_count + (own == named).astype(F32)
        far_count = far_count + (far_slot == named).astype(F32)
    own_count = own_count.astype(BF16)
    far_count = far_count * held_ref[...]
    far_ref[...] = far_count.astype(BF16)
    far_turned_ref[...] = far_count.T.astype(BF16)
    own_ref[...] = own_count
    features = features_ref[...]
    start_ref[...] = features.astype(F32) + dot(own_count, features, TN)


def prepare_kernel(
    candidates_hbm,
    noise_hbm,
    weight_hbm,
    candidates_ref,
    noise_ref,
    weight_ref,
    marks_ref,
    raw_noise_ref,
    sems,
):
    copies = start_copies(
        [(candidates_hbm, candidates_ref), (noise_hbm, raw_noise_ref), (weight_hbm, weight_ref)], sems
    )
    queries, cands = candidates_ref.shape
    blocks = cands // LANES
    samples = noise_ref.shape[0] // (queries * blocks)
    copies[0].wait()
    low = lax.bitwise_and(candidates_ref[...], jnp.int32(DIGIT - 1))
    for digit in range(DIGIT):
        marks_ref[digit * queries : (digit + 1) * queries, :] = (
            (low == digit).astype(F32).astype(BF16)
        )
    copies[1].wait()
    for m in range(samples):
        noise = [
            raw_noise_ref[pl.ds(j * samples + m, queries, stride=blocks * samples), :]
            for j in range(blocks)
        ]
        highest = jnp.max(functools.reduce(jnp.maximum, noise), axis=-1, keepdims=True)
        for j in range(blocks):
            at = (m * blocks + j) * queries
            noise_ref[at : at + queries, :] = jnp.exp(noise[j] - highest)
    copies[2].wait()


def main_kernel(
    towers,
    capacity,
    fanout,
    far_turned_ref,
    start_ref,
    candidates_ref,
    noise_ref,
    weight_ref,
    marks_ref,
    halo_kept_ref,
    halo_arrived_ref,
    *refs,
):
    *halo_refs, kept_turned_ref, sent_ref, d_pre_ref = refs
    *far_halo, passed, near = [ref[...].astype(F32) for ref in halo_refs]
    rows, width = start_ref.shape
    queries, cands = candidates_ref.shape
    samples = noise_ref.shape[0] // (queries * (cands // LANES))
    halo = slot_rows(halo_kept_ref[...], halo_arrived_ref[...], near, far_halo, passed, capacity)
    sums = start_ref[...] + dot(far_turned_ref[...], halo.astype(BF16), NN)
    mean_rows = (sums * (1.0 / (fanout + 1))).astype(BF16)

    tall = width // (2 * towers)
    turned = mean_rows.astype(F32).T
    tiles = slot_tiles([turned[i * tall : (i + 1) * tall] for i in range(2 * towers)])
    kept_turned, sent_turned = [
        jnp.concatenate([tiles[i] for i in slots], axis=0).astype(BF16)
        for slots in (kept_slots(towers), sent_slots(towers))
    ]

    weight = weight_ref[...]
    pre = dot(mean_rows, weight, NN)
    inverse = lax.rsqrt(jnp.mean(pre * pre, axis=-1, keepdims=True) + EPSILON)
    embedded = (pre * inverse).astype(BF16)
    factor = SCORE_SCALE / width
    rounded = pre.astype(BF16)
    similar = dot(rounded[:queries], rounded, NT)
    inverse_of_column = jnp.broadcast_to(inverse, (rows, rows)).T[:queries]
    similar = similar * (factor * inverse[:queries] * inverse_of_column)
    blocks = cands // LANES
    scores = [
        jnp.take_along_axis(similar, candidates_ref[:, j * LANES : (j + 1) * LANES], axis=1)
        for j in range(blocks)
    ]
    grown = [jnp.exp(x) for x in scores]
    soft = [jnp.zeros((queries, LANES), F32) for _ in range(blocks)]
    for m in range(samples):
        at = m * blocks * queries
        noise = [noise_ref[at + j * queries : at + (j + 1) * queries, :] for j in range(blocks)]
        total = jnp.sum(sum(n * g for n, g in zip(noise, grown)), axis=-1, keepdims=True)
        scale = (LOSS_SCALE * TOP / samples) / total
        soft = [a + n * scale for a, n in zip(soft, noise)]
    soft = [a * g for a, g in zip(soft, grown)]
    lane = lax.broadcasted_iota(jnp.int32, (queries, LANES), 1)
    d_scores = [
        jnp.where(lane + j * LANES < TOP, s - LOSS_SCALE, s) if j * LANES < TOP else s
        for j, s in enumerate(soft)
    ]
    d_scores = jnp.concatenate(d_scores, axis=1)

    high = candidates_ref[...] // DIGIT
    digits = rows // DIGIT
    weighted = [jnp.where(high == digit, d_scores, 0.0) for digit in range(digits)]
    crossed = dot(marks_ref[...], jnp.concatenate(weighted, axis=0).astype(BF16), NT)
    q_row = lax.broadcasted_iota(jnp.int32, crossed.shape, 0) % queries
    q_column = lax.broadcasted_iota(jnp.int32, crossed.shape, 1) % queries
    crossed = jnp.where(q_row == q_column, crossed, 0.0)
    kept = jnp.sum(crossed.reshape(DIGIT, queries, digits * queries), axis=1)
    d_similar = jnp.concatenate(
        [kept[:, i * queries : (i + 1) * queries] for i in range(digits)], axis=0
    ).astype(BF16)

    d_embedded = factor * dot(d_similar, embedded[:queries], NN)
    d_queries = factor * dot(d_similar, embedded, TN)
    d_embedded = jnp.concatenate(
        [d_embedded[:queries] + d_queries, d_embedded[queries:]], axis=0
    )
    inner = jnp.mean(d_embedded * pre, axis=-1, keepdims=True)
    d_pre = (inverse * d_embedded - inverse * inverse * inverse * pre * inner).astype(BF16)

    d_pre_ref[...] = d_pre
    sent_ref[...] = dot(sent_turned, d_pre, NN).astype(BF16)
    kept_turned_ref[...] = kept_turned


def own_term_kernel(kept_turned_ref, d_pre_ref, out_ref):
    out_ref[...] = dot(kept_turned_ref[...], d_pre_ref[...], NN)


def spread_kernel(
    towers, capacity, fanout, d_pre_ref, weight_ref, own_ref, far_ref, local_ref, kept_ref, sent_ref
):
    share = (dot(d_pre_ref[...], weight_ref[...], NT) * (1.0 / (fanout + 1))).astype(BF16)
    halo_grad = dot(far_ref[...], share, NN)
    kept_ref[...] = pick(halo_grad, kept_slots(towers), capacity)
    sent_ref[...] = pick(halo_grad, sent_slots(towers), capacity)
    local_ref[...] = share.astype(F32) + dot(own_ref[...], share, NN)


def core_sum_kernel(replicas, kept_ref, arrived_ref, own_ref, *out_refs):
    total = kept_ref[...] + arrived_ref[...].astype(F32)
    wide = total.shape[1] // replicas
    pieces = [total[:, r * wide : (r + 1) * wide] for r in range(replicas)]
    pieces = xor_order(pieces, lax.axis_index("replica"))
    own_ref[...] = pieces[0]
    for ref, piece in zip(out_refs, pieces[:0:-1]):
        ref[...] = piece.astype(BF16)


def store_block(ref, tiles, rows):
    high, wide = tiles.shape
    block = fold(rows)
    if (high + block.shape[0], wide) != ref.shape:
        ref[...] = jnp.zeros(ref.shape, ref.dtype)
    ref[0:high, 0:wide] = tiles.astype(ref.dtype)
    ref[ref.shape[0] - block.shape[0] :, :] = block.astype(ref.dtype)


def load_block(ref, high, wide, slots, parts):
    block = ref[...].astype(F32)
    return block[:high, :wide], unfold(block[block.shape[0] - slots * parts :], parts)


def replica_sum_kernel(replicas, capacity, *refs):
    term_refs, refs = refs[:replicas], refs[replicas:]
    kept_ref, arrived_ref, own_ref, near_ref, *far_refs = refs
    total = sum(ref[...].astype(F32) for ref in term_refs)
    tall = own_ref.shape[0]
    kept, arrived = kept_ref[...], arrived_ref[...]
    own_ref[...] = total[:tall]
    store_block(near_ref, total[tall : 2 * tall], near_rows(kept, arrived, capacity))
    for j, ref in enumerate(far_refs):
        tiles = total[2 * (j + 1) * tall : 2 * (j + 2) * tall]
        store_block(ref, tiles, far_rows(kept, arrived, j + 1, capacity))


def pass_sums_kernel(capacity, parts, tall, wide, *refs):
    far_refs, out_ref = refs[:-1], refs[-1]
    loaded = [load_block(ref, 2 * tall, wide, 4 * capacity, parts) for ref in far_refs]
    store_block(
        out_ref,
        sum(tiles[tall:] for tiles, _ in loaded),
        jnp.concatenate([pick(rows, [1, 3], capacity) for _, rows in loaded], axis=0),
    )


def final_kernel(capacity, devices, local_ref, onehot_ref, kept_ref, arrived_ref, own_ref, *refs):
    *far_refs, passed_ref, near_ref, features_out, weight_out = refs
    tall, wide = own_ref.shape
    parts = local_ref.shape[1] // LANES
    near_tile, near = load_block(near_ref, tall, wide, 2 * capacity, parts)
    loaded = [load_block(ref, 2 * tall, wide, 4 * capacity, parts) for ref in far_refs]
    passed_tile, passed = load_block(passed_ref, tall, wide, 2 * capacity * len(far_refs), parts)
    returned = slot_rows(
        kept_ref[...], arrived_ref[...], near, [rows for _, rows in loaded], passed, capacity
    )
    features_out[...] = (local_ref[...] + dot(onehot_ref[...], returned.astype(BF16), TN)).astype(BF16)
    total = own_ref[...] + near_tile + passed_tile + sum(tiles[:tall] for tiles, _ in loaded)
    weight_out[...] = total * (1.0 / math.sqrt(devices))


def body(features, neighbours, send_rows, send_counts, candidates, perturbation, weight):
    towers = lax.axis_size("z")
    replicas = lax.axis_size("replica")
    groups = 2 * towers
    devices = groups * replicas
    capacity = send_rows.shape[3]
    _, rows, width = features.shape
    _, queries, samples, cands = perturbation.shape
    fanout = neighbours.shape[2]
    slots = groups * capacity
    parts = width // LANES
    passes = towers // 2 - 1
    noise_rows = queries * samples * (cands // LANES)
    noise = (
        perturbation.reshape(queries, samples, cands // LANES, LANES)
        .transpose(0, 2, 1, 3)
        .reshape(noise_rows, LANES)
    )
    hbm = pl.BlockSpec(memory_space=pltpu.HBM)
    vmem = pl.BlockSpec(memory_space=pltpu.VMEM)
    shape = jax.ShapeDtypeStruct

    def call(kernel, name, operands, out_shape, from_hbm=(), scratch=()):
        from_hbm = [pltpu.with_memory_space_constraint(x, pltpu.HBM) for x in from_hbm]
        return pl.pallas_call(
            kernel,
            out_shape=out_shape,
            in_specs=[hbm] * len(from_hbm) + [vmem] * len(operands),
            out_specs=jax.tree.map(lambda _: vmem, out_shape),
            scratch_shapes=scratch,
            compiler_params=pltpu.CompilerParams(vmem_limit_bytes=32 * 1024 * 1024),
            name=name,
        )(*from_hbm, *operands)

    def swap_core(array):
        return lax.ppermute(array, "core", [(0, 1), (1, 0)])

    def swap_near(array):
        return lax.ppermute(array, "z", [(i, i ^ towers // 2) for i in range(towers)])

    def swap_far(arrays):
        return [
            lax.ppermute(
                array,
                ("z", "core"),
                [(2 * i + c, 2 * (i ^ j + c * towers // 2) + c) for i in range(towers) for c in range(2)],
            )
            for j, array in enumerate(arrays, 1)
        ]

    def swap_replica(arrays):
        return [
            lax.ppermute(array, "replica", [(i, i ^ s) for i in range(replicas)])
            for array, s in zip(arrays, range(replicas - 1, 0, -1))
        ]

    half = shape((slots // 2, width), F32)
    kept, sent, onehot, held, feature_rows, neighbour_rows = call(
        functools.partial(outgoing_kernel, towers, capacity),
        "outgoing",
        [],
        [
            half,
            half,
            shape((slots, rows), BF16),
            shape((slots, rows), F32),
            shape((rows, width), BF16),
            shape((fanout, rows), jnp.int32),
        ],
        [
            jnp.swapaxes(send_rows[0, 0], 0, 1),
            send_counts[0],
            features[0],
            jnp.swapaxes(neighbours[0], 0, 1),
        ],
        (
            pltpu.SMEM((capacity, groups), jnp.int32),
            pltpu.SMEM((1, groups), jnp.int32),
            pltpu.SemaphoreType.DMA((4,)),
        ),
    )
    arrived = swap_core(sent)
    own, far, far_turned, start = call(
        functools.partial(adjacency_kernel, towers, capacity),
        "adjacency",
        [held, feature_rows, neighbour_rows],
        [
            shape((rows, rows), BF16),
            shape((slots, rows), BF16),
            shape((rows, slots), BF16),
            shape((rows, width), F32),
        ],
    )
    near, *far_sent = call(
        functools.partial(hop_kernel, capacity),
        "halo_hop",
        [far, kept, arrived],
        [shape((2 * capacity, width), BF16)] + [shape((4 * capacity, width), BF16)] * passes,
    )
    far_halo = swap_far(far_sent)
    near = swap_near(near)
    passed = swap_core(
        call(
            functools.partial(pass_kernel, capacity),
            "halo_pass",
            far_halo,
            shape((2 * capacity * passes, width), BF16),
        )
    )
    candidate_rows, noise, weight, marks = call(
        prepare_kernel,
        "prepare",
        [],
        [
            shape((queries, cands), jnp.int32),
            shape((noise_rows, LANES), F32),
            shape((width, width), BF16),
            shape((DIGIT * queries, cands), BF16),
        ],
        [candidates[0], noise, weight],
        (pltpu.VMEM((noise_rows, LANES), F32), pltpu.SemaphoreType.DMA((3,))),
    )
    kept_turned, sent, d_pre = call(
        functools.partial(main_kernel, towers, capacity, fanout),
        "forward_backward",
        [far_turned, start, candidate_rows, noise, weight, marks, kept, arrived, *far_halo, passed, near],
        [
            shape((width // 2, rows), BF16),
            shape((width // 2, width), BF16),
            shape((rows, width), BF16),
        ],
    )

    arrived = swap_core(sent)
    kept = call(own_term_kernel, "own_term", [kept_turned, d_pre], shape((width // 2, width), F32))
    local, halo_kept, halo_sent = call(
        functools.partial(spread_kernel, towers, capacity, fanout),
        "spread",
        [d_pre, weight, own, far],
        [shape((rows, width), F32), half, half],
    )
    halo_arrived = swap_core(halo_sent)
    tall, wide = width // groups, width // replicas
    own_term, *terms = call(
        functools.partial(core_sum_kernel, replicas),
        "core_sum",
        [kept, arrived],
        [shape((width // 2, wide), F32)] + [shape((width // 2, wide), BF16)] * (replicas - 1),
    )
    terms = swap_replica(terms)

    def block(tiles, slot_count, dtype):
        return shape((-(-tiles * tall // 16) * 16 + slot_count * capacity * parts, LANES), dtype)

    own_tile, near, *far_sent = call(
        functools.partial(replica_sum_kernel, replicas, capacity),
        "replica_sum",
        [own_term, *terms, halo_kept, halo_arrived],
        [shape((tall, wide), F32), block(1, 2, BF16)] + [block(2, 4, BF16)] * passes,
    )
    far_sums = swap_far(far_sent)
    near = swap_near(near)
    passed = swap_core(
        call(
            functools.partial(pass_sums_kernel, capacity, parts, tall, wide),
            "pass_sums",
            far_sums,
            block(1, 2 * passes, BF16),
        )
    )
    d_features, weight_grad = call(
        functools.partial(final_kernel, capacity, devices),
        "final",
        [local, onehot, halo_kept, halo_arrived, own_tile, *far_sums, passed, near],
        [shape((rows, width), BF16), shape((tall, wide), F32)],
    )
    return (d_features[None], weight_grad)


def solution(mesh):
    groups, replicas = mesh.devices.shape
    split = jax.sharding.Mesh(
        mesh.devices.reshape(groups // 2, 2, replicas), ("z", "core", "replica")
    )
    graph = ("z", "core")
    placed = (
        P("replica", graph, None),
        P("replica", graph, None),
        P("replica", graph, None, None),
        P("replica", graph, None),
        P("replica", graph, None),
        P("replica", graph, None, None),
        P(),
    )
    return jax.shard_map(
        body,
        mesh=split,
        in_specs=placed,
        out_specs=(P("replica", graph, None), P(graph, "replica")),
        check_vma=False,
    )
```

time: 306 us -> 28.4 us (0.09)
  other arithmetic: 120 us -> 0 us
  local copies, waits for them, and re-layouts: 106 us -> 0 us
  waiting for transfers between devices: 52 us -> 6.96 us
  between operations: 14.3 us -> 0.72 us
  Pallas kernels: 0 us -> 6.09 us
  starting transfers between devices: 10.1 us -> 14.4 us
  matrix products: 3.45 us -> 0 us
    unnamed x6 -> x0, other arithmetic: 116 us -> none
    gather x3 -> x0, local copies, waits for them, and re-layouts: 102 us -> none  [the longest x2 101 us: embed_backward(): scores = factor * jnp.take_along_axis(similar, candidates, axis=1)]
    reduce_scatter x2 -> x0, waiting for transfers between devices: 50.5 us -> none  [the longest x1 27.6 us: body(): lax.psum_scatter(lax.dot_general(mean_rows, d_pre, (((0,), (0,)), ((), ()...]
    ppermute x0 -> x12, starting transfers between devices: none -> 14.4 us  [the longest x2 5.79 us: swap_near(): lax.ppermute(array, 'z', [(i, i ^ towers // 2) for i in range(towers)])]
    all_to_all x2 -> x0, starting transfers between devices: 9.99 us -> none  [the longest x1 6.33 us: body(): lax.all_to_all(outgoing, 'graph', split_axis=0, concat_axis=0, tiled=True)]
    ppermute x0 -> x12, waiting for transfers between devices: none -> 6.96 us  [the longest x5 2.96 us: swap_core(): return lax.ppermute(array, 'core', [(0, 1), (1, 0)])]
    pallas_call x0 -> x12, Pallas kernels: none -> 6.09 us  [call(): pl.pallas_call(kernel, out_shape=out_shape, in_specs=[hbm] * len(from_hbm...]
    dot_general x8 -> x0, matrix products: 3.45 us -> none  [the longest x1 1.31 us: body(): lax.dot_general(mean_rows, d_pre, (((0,), (0,)), ((), ())), preferred_ele...]
  transfers between devices with their start and end apart: 4 -> 12, of which waited for: 3 -> 9; matrix products, arithmetic and copies ran while one was open for 2% -> 0% of each run, Pallas kernels for 0% -> 8%
where the time goes in v1:
time: 28.4 us; the launch traced here: 28.2 us
  starting transfers between devices  14.4 us (51%)
  waiting for transfers between devices  6.96 us (25%)
  Pallas kernels  6.09 us (21%)
  between operations  0.72 us (3%)
    pallas_call x12, Pallas kernels, call(): pl.pallas_call(kernel, out_shape=out_shape, in_specs=[hbm] * len(from_hbm...  6.09 us
    ppermute x2, starting transfers between devices, swap_near(): lax.ppermute(array, 'z', [(i, i ^ towers // 2) for i in range(towers)])  5.79 us
    ppermute x3, starting transfers between devices, swap_replica(): lax.ppermute(array, 'replica', [(i, i ^ s) for i in range(replicas)])  3.57 us
    ppermute x2, starting transfers between devices, swap_far(): lax.ppermute(array, ('z', 'core'), [(2 * i + c, 2 * (i ^ j + c * towers /...  3.27 us
    ppermute x5, waiting for transfers between devices, swap_core(): return lax.ppermute(array, 'core', [(0, 1), (1, 0)])  2.96 us
    ppermute x3, waiting for transfers between devices, swap_replica(): lax.ppermute(array, 'replica', [(i, i ^ s) for i in range(replicas)])  1.99 us
    ppermute x5, starting transfers between devices, swap_core(): return lax.ppermute(array, 'core', [(0, 1), (1, 0)])  1.81 us
    ppermute x2, waiting for transfers between devices, swap_near(): lax.ppermute(array, 'z', [(i, i ^ towers // 2) for i in range(towers)])  1.22 us
  transfers between devices with their start and end apart: 12, of which 9 were waited for; matrix products, arithmetic and copies ran while one was open for 0% of the time, Pallas kernels for 8%

profile of v1, /device:TPU:0, one launch (start us, length us, event | category | flops | bytes accessed | tf_op | source)
XLA Modules:
  0.0 28.2 jit_solution(9244740985479218159)
XLA Ops:
  0.6 1.1 %outgoing.1 = (f32[8,512]{1,0:T(8,128)S(1)}, f32[8,512]{1,0:T(8,128)S(1)}, bf16[16,128]{1,0:T(8,128)(2,1)S(1)}, f32[16,128]{1,0:T(8,128)S(1)}, bf16[128,512]{1,0:T(8,128)(2,1)S(1)}, /*index=5*/s32[16,128]{1,0:T(8,128)S(1)}) custom-call(s32[2,8]{1,0:T(2,128)} %bitcast.19, s32[1,8]{1,0:T(1,128)} %bitcast.20, bf16[128,512]{1,0:T(8,128)(2,1)} %bitcast.16, ...), custom_call_target="tpu_custom_call" | custom-call | tf_op jit(solution)/shard_map/outgoing/pallas_call | solution.py:421
  1.7 0.5 %collective-permute-start = (f32[8,512]{1,0:T(8,128)S(1)}, f32[8,512]{1,0:T(8,128)S(1)}, u32[]{:S(2)}, u32[]{:S(2)}) collective-permute-start(f32[8,512]{1,0:T(8,128)S(1)} %get-tuple-element.43), channel_id=1, source_target_pairs={{0,4},{4,0},{1,5},{5,1},{2,6},{6,2},{3,7},{7,3},{8,12},{12,8},{9,1... | collective-permute-start | bytes 49160 | tf_op jit(solution)/shard_map/ppermute | solution.py:432
  2.2 0.3 %adjacency.1 = (bf16[128,128]{1,0:T(8,128)(2,1)S(1)}, bf16[16,128]{1,0:T(8,128)(2,1)S(1)}, bf16[128,16]{1,0:T(8,128)(2,1)S(1)}, f32[128,512]{1,0:T(8,128)S(1)}) custom-call(f32[16,128]{1,0:T(8,128)S(1)} %get-tuple-element.33.held_ref, bf16[128,512]{1,0:T(8,128)(2,1)S(1)} %get-tuple-element.34.features_ref, s32[16,128]{1,0:T(8,128)S(1)} %get-tuple-element.35.neighbours_ref), custom_call_target="tpu_custom_call" | custom-call | tf_op jit(solution)/shard_map/adjacency/pallas_call | solution.py:421
  2.5 0.5 %collective-permute-done.arrived_ref.halo_arrived_ref = f32[8,512]{1,0:T(8,128)S(1)} collective-permute-done((f32[8,512]{1,0:T(8,128)S(1)}, f32[8,512]{1,0:T(8,128)S(1)}, u32[]{:S(2)}, u32[]{:S(2)}) %collective-permute-start) | collective-permute-done | bytes 16416 | tf_op jit(solution)/shard_map/ppermute | solution.py:432
  3.1 3.0 %collective-permute-start.1 = (bf16[8,512]{1,0:T(8,128)(2,1)S(1)}, bf16[8,512]{1,0:T(8,128)(2,1)S(1)}, u32[]{:S(2)}, u32[]{:S(2)}) collective-permute-start(bf16[8,512]{1,0:T(8,128)(2,1)S(1)} %get-tuple-element.45), channel_id=1, source_target_pairs={{0,8},{4,28},{8,0},{12,20},{16,24},{20,12},{24,16},{28,4},{1,9},{5... | collective-permute-start | bytes 24584 | tf_op jit(solution)/shard_map/ppermute | solution.py:439
  6.1 2.6 %collective-permute-start.3 = (bf16[4,512]{1,0:T(4,128)(2,1)S(1)}, bf16[4,512]{1,0:T(4,128)(2,1)S(1)}, u32[]{:S(2)}, u32[]{:S(2)}) collective-permute-start(bf16[4,512]{1,0:T(4,128)(2,1)S(1)} %get-tuple-element.46), channel_id=1, source_target_pairs={{0,16},{8,24},{16,0},{24,8},{1,17},{9,25},{17,1},{25,9},{2,18},{10... | collective-permute-start | bytes 12296 | tf_op jit(solution)/shard_map/ppermute | solution.py:435
  8.7 0.4 %collective-permute-start.2 = (bf16[4,512]{1,0:T(4,128)(2,1)S(1)}, bf16[4,512]{1,0:T(4,128)(2,1)S(1)}, u32[]{:S(2)}, u32[]{:S(2)}) collective-permute-start(bf16[4,512]{1,0:T(4,128)(2,1)S(1)} %halo_pass.1), channel_id=1, source_target_pairs={{0,4},{4,0},{1,5},{5,1},{2,6},{6,2},{3,7},{7,3},{8,12},{12,8},{9,1... | collective-permute-start | bytes 12296 | tf_op jit(solution)/shard_map/ppermute | solution.py:432
  9.0 1.2 %prepare.1 = (s32[32,512]{1,0:T(8,128)S(1)}, f32[512,128]{1,0:T(8,128)S(1)}, bf16[512,512]{1,0:T(8,128)(2,1)S(1)}, bf16[512,512]{1,0:T(8,128)(2,1)S(1)}) custom-call(s32[32,512]{1,0:T(8,128)} %bitcast.17, f32[512,128]{1,0:T(8,128)} %bitcast.15, bf16[512,512]{1,0:T(8,128)(2,1)} %weight_hbm.1), custom_call_target="tpu_custom_call" | custom-call | tf_op jit(solution)/shard_map/prepare/pallas_call | solution.py:421
  10.2 0.3 %collective-permute-done.3.refs_2_ = bf16[4,512]{1,0:T(4,128)(2,1)S(1)} collective-permute-done((bf16[4,512]{1,0:T(4,128)(2,1)S(1)}, bf16[4,512]{1,0:T(4,128)(2,1)S(1)}, u32[]{:S(2)}, u32[]{:S(2)}) %collective-permute-start.3) | collective-permute-done | bytes 4128 | tf_op jit(solution)/shard_map/ppermute | solution.py:435
  10.6 1.8 %forward_backward.1 = (bf16[256,128]{1,0:T(8,128)(2,1)S(1)}, bf16[256,512]{1,0:T(8,128)(2,1)S(1)}, bf16[128,512]{1,0:T(8,128)(2,1)S(1)}) custom-call(bf16[128,16]{1,0:T(8,128)(2,1)S(1)} %get-tuple-element.36.far_turned_ref, f32[128,512]{1,0:T(8,128)S(1)} %get-tuple-element.37.start_ref, s32[32,512]{1,0:T(8,128)S(1)} %get-tuple-element.38.candidates_ref, ...), custom_call_target="tpu_custom_call" | custom-call | tf_op jit(solution)/shard_map/forward_backward/pallas_call | solution.py:421
  12.4 0.8 %collective-permute-start.5 = (bf16[256,512]{1,0:T(8,128)(2,1)S(1)}, bf16[256,512]{1,0:T(8,128)(2,1)S(1)}, u32[]{:S(2)}, u32[]{:S(2)}) collective-permute-start(bf16[256,512]{1,0:T(8,128)(2,1)S(1)} %get-tuple-element.54), channel_id=1, source_target_pairs={{0,4},{4,0},{1,5},{5,1},{2,6},{6,2},{3,7},{7,3},{8,12},{12,8},{9,1... | collective-permute-start | bytes 786440 | tf_op jit(solution)/shard_map/ppermute | solution.py:432
  13.4 1.0 %collective-permute-done.5.arrived_ref = bf16[256,512]{1,0:T(8,128)(2,1)S(1)} collective-permute-done((bf16[256,512]{1,0:T(8,128)(2,1)S(1)}, bf16[256,512]{1,0:T(8,128)(2,1)S(1)}, u32[]{:S(2)}, u32[]{:S(2)}) %collective-permute-start.5) | collective-permute-done | bytes 262176 | tf_op jit(solution)/shard_map/ppermute | solution.py:432
  14.4 2.5 %collective-permute-start.6 = (bf16[256,128]{1,0:T(8,128)(2,1)S(1)}, bf16[256,128]{1,0:T(8,128)(2,1)S(1)}, u32[]{:S(2)}, u32[]{:S(2)}) collective-permute-start(bf16[256,128]{1,0:T(8,128)(2,1)S(1)} %get-tuple-element.56), channel_id=1, source_target_pairs={{0,3},{1,2},{2,1},{3,0},{4,7},{5,6},{6,5},{7,4},{8,11},{9,10},{10,... | collective-permute-start | bytes 196616 | tf_op jit(solution)/shard_map/ppermute | solution.py:449
  17.0 0.5 %collective-permute-start.7 = (bf16[256,128]{1,0:T(8,128)(2,1)S(1)}, bf16[256,128]{1,0:T(8,128)(2,1)S(1)}, u32[]{:S(2)}, u32[]{:S(2)}) collective-permute-start(bf16[256,128]{1,0:T(8,128)(2,1)S(1)} %get-tuple-element.57), channel_id=1, source_target_pairs={{0,2},{1,3},{2,0},{3,1},{4,6},{5,7},{6,4},{7,5},{8,10},{9,11},{10,... | collective-permute-start | bytes 196616 | tf_op jit(solution)/shard_map/ppermute | solution.py:449
  17.5 0.5 %collective-permute-start.8 = (bf16[256,128]{1,0:T(8,128)(2,1)S(1)}, bf16[256,128]{1,0:T(8,128)(2,1)S(1)}, u32[]{:S(2)}, u32[]{:S(2)}) collective-permute-start(bf16[256,128]{1,0:T(8,128)(2,1)S(1)} %get-tuple-element.58), channel_id=1, source_target_pairs={{0,1},{1,0},{2,3},{3,2},{4,5},{5,4},{6,7},{7,6},{8,9},{9,8},{10,11... | collective-permute-start | bytes 196616 | tf_op jit(solution)/shard_map/ppermute | solution.py:449
  18.0 0.5 %spread.1 = (f32[128,512]{1,0:T(8,128)S(1)}, f32[8,512]{1,0:T(8,128)S(1)}, f32[8,512]{1,0:T(8,128)S(1)}) custom-call(bf16[128,512]{1,0:T(8,128)(2,1)S(1)} %get-tuple-element.47.d_pre_ref, bf16[512,512]{1,0:T(8,128)(2,1)S(1)} %get-tuple-element.40.weight_ref, bf16[128,128]{1,0:T(8,128)(2,1)S(1)} %get-tuple-element.48.own_ref, ...), custom_call_target="tpu_custom_call" | custom-call | tf_op jit(solution)/shard_map/spread/pallas_call | solution.py:421
  18.6 1.2 %collective-permute-done.4.refs_5_.arrived_ref = f32[8,512]{1,0:T(8,128)S(1)} collective-permute-done((f32[8,512]{1,0:T(8,128)S(1)}, f32[8,512]{1,0:T(8,128)S(1)}, u32[]{:S(2)}, u32[]{:S(2)}) %collective-permute-start.4) | collective-permute-done | bytes 16416 | tf_op jit(solution)/shard_map/ppermute | solution.py:432
  19.8 1.4 %collective-permute-done.7.refs_2_ = bf16[256,128]{1,0:T(8,128)(2,1)S(1)} collective-permute-done((bf16[256,128]{1,0:T(8,128)(2,1)S(1)}, bf16[256,128]{1,0:T(8,128)(2,1)S(1)}, u32[]{:S(2)}, u32[]{:S(2)}) %collective-permute-start.7) | collective-permute-done | bytes 65568 | tf_op jit(solution)/shard_map/ppermute | solution.py:449
  21.2 0.5 %collective-permute-done.8.refs_3_ = bf16[256,128]{1,0:T(8,128)(2,1)S(1)} collective-permute-done((bf16[256,128]{1,0:T(8,128)(2,1)S(1)}, bf16[256,128]{1,0:T(8,128)(2,1)S(1)}, u32[]{:S(2)}, u32[]{:S(2)}) %collective-permute-start.8) | collective-permute-done | bytes 65568 | tf_op jit(solution)/shard_map/ppermute | solution.py:449
  22.1 3.2 %collective-permute-start.11 = (bf16[80,128]{1,0:T(8,128)(2,1)S(1)}, bf16[80,128]{1,0:T(8,128)(2,1)S(1)}, u32[]{:S(2)}, u32[]{:S(2)}) collective-permute-start(bf16[80,128]{1,0:T(8,128)(2,1)S(1)} %get-tuple-element.61), channel_id=1, source_target_pairs={{0,16},{8,24},{16,0},{24,8},{1,17},{9,25},{17,1},{25,9},{2,18},{10... | collective-permute-start | bytes 61448 | tf_op jit(solution)/shard_map/ppermute | solution.py:435
  25.3 0.8 %collective-permute-done.9.refs_0_ = bf16[160,128]{1,0:T(8,128)(2,1)S(1)} collective-permute-done((bf16[160,128]{1,0:T(8,128)(2,1)S(1)}, bf16[160,128]{1,0:T(8,128)(2,1)S(1)}, u32[]{:S(2)}, u32[]{:S(2)}) %collective-permute-start.9) | collective-permute-done | bytes 40992 | tf_op jit(solution)/shard_map/ppermute | solution.py:439
  26.2 0.9 %collective-permute-done.11.refs_2_ = bf16[80,128]{1,0:T(8,128)(2,1)S(1)} collective-permute-done((bf16[80,128]{1,0:T(8,128)(2,1)S(1)}, bf16[80,128]{1,0:T(8,128)(2,1)S(1)}, u32[]{:S(2)}, u32[]{:S(2)}) %collective-permute-start.11) | collective-permute-done | bytes 20512 | tf_op jit(solution)/shard_map/ppermute | solution.py:435
  27.0 0.3 %collective-permute-done.10.refs_1_ = bf16[80,128]{1,0:T(8,128)(2,1)S(1)} collective-permute-done((bf16[80,128]{1,0:T(8,128)(2,1)S(1)}, bf16[80,128]{1,0:T(8,128)(2,1)S(1)}, u32[]{:S(2)}, u32[]{:S(2)}) %collective-permute-start.10) | collective-permute-done | bytes 20512 | tf_op jit(solution)/shard_map/ppermute | solution.py:432
  27.3 0.9 %final.1 = (bf16[128,512]{1,0:T(8,128)(2,1)}, f32[64,128]{1,0:T(8,128)}) custom-call(f32[128,512]{1,0:T(8,128)S(1)} %get-tuple-element.49.local_ref, bf16[16,128]{1,0:T(8,128)(2,1)S(1)} %get-tuple-element.50.onehot_ref, f32[8,512]{1,0:T(8,128)S(1)} %get-tuple-element.51.refs_4_.kept_ref, f32[8,512]{1,0:T(8,128)S(1)} %collective-permute-done.4.refs_5_.arrived_ref, ...), custom_call_target="tpu_custom_call" | custom-call | tf_op jit(solution)/shard_map/final/pallas_call | solution.py:421
  (12 shorter events, 0.8 us)
Async XLA Ops:
  1.7 1.4 %collective-permute-start = (f32[8,512]{1,0:T(8,128)S(1)}, f32[8,512]{1,0:T(8,128)S(1)}, u32[]{:S(2)}, u32[]{:S(2)}) collective-permute-start(f32[8,512]{1,0:T(8,128)S(1)} %get-tuple-element.43), channel_id=1, source_target_pairs={{0,4},{4,0},{1,5},{5,1},{2,6},{6,2},{3,7},{7,3},{8,12},{12,8},{9,1... | collective-permute-start | bytes 49160 | tf_op jit(solution)/shard_map/ppermute | solution.py:432
  3.1 5.6 %collective-permute-start.1 = (bf16[8,512]{1,0:T(8,128)(2,1)S(1)}, bf16[8,512]{1,0:T(8,128)(2,1)S(1)}, u32[]{:S(2)}, u32[]{:S(2)}) collective-permute-start(bf16[8,512]{1,0:T(8,128)(2,1)S(1)} %get-tuple-element.45), channel_id=1, source_target_pairs={{0,8},{4,28},{8,0},{12,20},{16,24},{20,12},{24,16},{28,4},{1,9},{5... | collective-permute-start | bytes 24584 | tf_op jit(solution)/shard_map/ppermute | solution.py:439
  6.1 4.5 %collective-permute-start.3 = (bf16[4,512]{1,0:T(4,128)(2,1)S(1)}, bf16[4,512]{1,0:T(4,128)(2,1)S(1)}, u32[]{:S(2)}, u32[]{:S(2)}) collective-permute-start(bf16[4,512]{1,0:T(4,128)(2,1)S(1)} %get-tuple-element.46), channel_id=1, source_target_pairs={{0,16},{8,24},{16,0},{24,8},{1,17},{9,25},{17,1},{25,9},{2,18},{10... | collective-permute-start | bytes 12296 | tf_op jit(solution)/shard_map/ppermute | solution.py:435
  8.7 1.9 %collective-permute-start.2 = (bf16[4,512]{1,0:T(4,128)(2,1)S(1)}, bf16[4,512]{1,0:T(4,128)(2,1)S(1)}, u32[]{:S(2)}, u32[]{:S(2)}) collective-permute-start(bf16[4,512]{1,0:T(4,128)(2,1)S(1)} %halo_pass.1), channel_id=1, source_target_pairs={{0,4},{4,0},{1,5},{5,1},{2,6},{6,2},{3,7},{7,3},{8,12},{12,8},{9,1... | collective-permute-start | bytes 12296 | tf_op jit(solution)/shard_map/ppermute | solution.py:432
  12.4 1.9 %collective-permute-start.5 = (bf16[256,512]{1,0:T(8,128)(2,1)S(1)}, bf16[256,512]{1,0:T(8,128)(2,1)S(1)}, u32[]{:S(2)}, u32[]{:S(2)}) collective-permute-start(bf16[256,512]{1,0:T(8,128)(2,1)S(1)} %get-tuple-element.54), channel_id=1, source_target_pairs={{0,4},{4,0},{1,5},{5,1},{2,6},{6,2},{3,7},{7,3},{8,12},{12,8},{9,1... | collective-permute-start | bytes 786440 | tf_op jit(solution)/shard_map/ppermute | solution.py:432
  14.4 5.3 %collective-permute-start.6 = (bf16[256,128]{1,0:T(8,128)(2,1)S(1)}, bf16[256,128]{1,0:T(8,128)(2,1)S(1)}, u32[]{:S(2)}, u32[]{:S(2)}) collective-permute-start(bf16[256,128]{1,0:T(8,128)(2,1)S(1)} %get-tuple-element.56), channel_id=1, source_target_pairs={{0,3},{1,2},{2,1},{3,0},{4,7},{5,6},{6,5},{7,4},{8,11},{9,10},{10,... | collective-permute-start | bytes 196616 | tf_op jit(solution)/shard_map/ppermute | solution.py:449
  17.0 4.3 %collective-permute-start.7 = (bf16[256,128]{1,0:T(8,128)(2,1)S(1)}, bf16[256,128]{1,0:T(8,128)(2,1)S(1)}, u32[]{:S(2)}, u32[]{:S(2)}) collective-permute-start(bf16[256,128]{1,0:T(8,128)(2,1)S(1)} %get-tuple-element.57), channel_id=1, source_target_pairs={{0,2},{1,3},{2,0},{3,1},{4,6},{5,7},{6,4},{7,5},{8,10},{9,11},{10,... | collective-permute-start | bytes 196616 | tf_op jit(solution)/shard_map/ppermute | solution.py:449
  17.5 4.3 %collective-permute-start.8 = (bf16[256,128]{1,0:T(8,128)(2,1)S(1)}, bf16[256,128]{1,0:T(8,128)(2,1)S(1)}, u32[]{:S(2)}, u32[]{:S(2)}) collective-permute-start(bf16[256,128]{1,0:T(8,128)(2,1)S(1)} %get-tuple-element.58), channel_id=1, source_target_pairs={{0,1},{1,0},{2,3},{3,2},{4,5},{5,4},{6,7},{7,6},{8,9},{9,8},{10,11... | collective-permute-start | bytes 196616 | tf_op jit(solution)/shard_map/ppermute | solution.py:449
  18.5 1.2 %collective-permute-start.4 = (f32[8,512]{1,0:T(8,128)S(1)}, f32[8,512]{1,0:T(8,128)S(1)}, u32[]{:S(2)}, u32[]{:S(2)}) collective-permute-start(f32[8,512]{1,0:T(8,128)S(1)} %get-tuple-element.52), channel_id=1, source_target_pairs={{0,4},{4,0},{1,5},{5,1},{2,6},{6,2},{3,7},{7,3},{8,12},{12,8},{9,1... | collective-permute-start | bytes 49160 | tf_op jit(solution)/shard_map/ppermute | solution.py:432
  21.8 4.3 %collective-permute-start.9 = (bf16[160,128]{1,0:T(8,128)(2,1)S(1)}, bf16[160,128]{1,0:T(8,128)(2,1)S(1)}, u32[]{:S(2)}, u32[]{:S(2)}) collective-permute-start(bf16[160,128]{1,0:T(8,128)(2,1)S(1)} %get-tuple-element.60), channel_id=1, source_target_pairs={{0,8},{4,28},{8,0},{12,20},{16,24},{20,12},{24,16},{28,4},{1,9},{5... | collective-permute-start | bytes 122888 | tf_op jit(solution)/shard_map/ppermute | solution.py:439
  22.1 5.0 %collective-permute-start.11 = (bf16[80,128]{1,0:T(8,128)(2,1)S(1)}, bf16[80,128]{1,0:T(8,128)(2,1)S(1)}, u32[]{:S(2)}, u32[]{:S(2)}) collective-permute-start(bf16[80,128]{1,0:T(8,128)(2,1)S(1)} %get-tuple-element.61), channel_id=1, source_target_pairs={{0,16},{8,24},{16,0},{24,8},{1,17},{9,25},{17,1},{25,9},{2,18},{10... | collective-permute-start | bytes 61448 | tf_op jit(solution)/shard_map/ppermute | solution.py:435
  26.1 1.3 %collective-permute-start.10 = (bf16[80,128]{1,0:T(8,128)(2,1)S(1)}, bf16[80,128]{1,0:T(8,128)(2,1)S(1)}, u32[]{:S(2)}, u32[]{:S(2)}) collective-permute-start(bf16[80,128]{1,0:T(8,128)(2,1)S(1)} %pass_sums.1), channel_id=1, source_target_pairs={{0,4},{4,0},{1,5},{5,1},{2,6},{6,2},{3,7},{7,3},{8,12},{12,8},{9,1... | collective-permute-start | bytes 61448 | tf_op jit(solution)/shard_map/ppermute | solution.py:432

commit v2 on v1

--- a/solution.py
+++ b/solution.py
@@ -109,12 +109,16 @@
     counts_hbm,
     features_hbm,
     neighbours_hbm,
+    candidates_hbm,
+    noise_hbm,
     kept_ref,
     sent_ref,
     onehot_ref,
     held_ref,
     features_ref,
     neighbours_ref,
+    candidates_ref,
+    noise_ref,
     send_smem,
     counts_smem,
     sems,
@@ -125,6 +129,8 @@
             (counts_hbm, counts_smem),
             (features_hbm, features_ref),
             (neighbours_hbm, neighbours_ref),
+            (candidates_hbm, candidates_ref),
+            (noise_hbm, noise_ref),
         ],
         sems,
     )
@@ -148,7 +154,8 @@
     picked = dot(onehot, features_ref[...], NN)
     kept_ref[...] = pick(picked, kept_slots(towers), capacity)
     sent_ref[...] = pick(picked, sent_slots(towers), capacity)
-    copies[3].wait()
+    for copy in copies[3:]:
+        copy.wait()
 
 
 def hop_kernel(capacity, after_ref, kept_ref, arrived_ref, near_ref, *far_refs):
@@ -164,16 +171,20 @@
     out_ref[...] = jnp.concatenate(rows, axis=0).astype(BF16)
 
 
-def adjacency_kernel(
+def prepare_kernel(
     towers,
     capacity,
     held_ref,
     features_ref,
     neighbours_ref,
+    candidates_ref,
+    raw_noise_ref,
     own_ref,
     far_ref,
     far_turned_ref,
     start_ref,
+    marks_ref,
+    noise_ref,
 ):
     rows = features_ref.shape[0]
     fanout = neighbours_ref.shape[0]
@@ -194,32 +205,14 @@
     own_ref[...] = own_count
     features = features_ref[...]
     start_ref[...] = features.astype(F32) + dot(own_count, features, TN)
-
-
-def prepare_kernel(
-    candidates_hbm,
-    noise_hbm,
-    weight_hbm,
-    candidates_ref,
-    noise_ref,
-    weight_ref,
-    marks_ref,
-    raw_noise_ref,
-    sems,
-):
-    copies = start_copies(
-        [(candidates_hbm, candidates_ref), (noise_hbm, raw_noise_ref), (weight_hbm, weight_ref)], sems
-    )
     queries, cands = candidates_ref.shape
     blocks = cands // LANES
     samples = noise_ref.shape[0] // (queries * blocks)
-    copies[0].wait()
     low = lax.bitwise_and(candidates_ref[...], jnp.int32(DIGIT - 1))
     for digit in range(DIGIT):
         marks_ref[digit * queries : (digit + 1) * queries, :] = (
             (low == digit).astype(F32).astype(BF16)
         )
-    copies[1].wait()
     for m in range(samples):
         noise = [
             raw_noise_ref[pl.ds(j * samples + m, queries, stride=blocks * samples), :]
@@ -229,7 +222,12 @@
         for j in range(blocks):
             at = (m * blocks + j) * queries
             noise_ref[at : at + queries, :] = jnp.exp(noise[j] - highest)
-    copies[2].wait()
+
+
+def weight_kernel(weight_hbm, weight_ref, sem):
+    copy = pltpu.make_async_copy(weight_hbm, weight_ref, sem)
+    copy.start()
+    copy.wait()
 
 
 def main_kernel(
@@ -451,7 +449,7 @@
         ]
 
     half = shape((slots // 2, width), F32)
-    kept, sent, onehot, held, feature_rows, neighbour_rows = call(
+    kept, sent, onehot, held, feature_rows, neighbour_rows, candidate_rows, noise = call(
         functools.partial(outgoing_kernel, towers, capacity),
         "outgoing",
         [],
@@ -462,29 +460,35 @@
             shape((slots, rows), F32),
             shape((rows, width), BF16),
             shape((fanout, rows), jnp.int32),
+            shape((queries, cands), jnp.int32),
+            shape((noise_rows, LANES), F32),
         ],
         [
             jnp.swapaxes(send_rows[0, 0], 0, 1),
             send_counts[0],
             features[0],
             jnp.swapaxes(neighbours[0], 0, 1),
+            candidates[0],
+            noise,
         ],
         (
             pltpu.SMEM((capacity, groups), jnp.int32),
             pltpu.SMEM((1, groups), jnp.int32),
-            pltpu.SemaphoreType.DMA((4,)),
+            pltpu.SemaphoreType.DMA((6,)),
         ),
     )
     arrived = swap_core(sent)
-    own, far, far_turned, start = call(
-        functools.partial(adjacency_kernel, towers, capacity),
-        "adjacency",
-        [held, feature_rows, neighbour_rows],
+    own, far, far_turned, start, marks, noise = call(
+        functools.partial(prepare_kernel, towers, capacity),
+        "prepare",
+        [held, feature_rows, neighbour_rows, candidate_rows, noise],
         [
             shape((rows, rows), BF16),
             shape((slots, rows), BF16),
             shape((rows, slots), BF16),
             shape((rows, width), F32),
+            shape((DIGIT * queries, cands), BF16),
+            shape((noise_rows, LANES), F32),
         ],
     )
     near, *far_sent = call(
@@ -503,18 +507,13 @@
             shape((2 * capacity * passes, width), BF16),
         )
     )
-    candidate_rows, noise, weight, marks = call(
-        prepare_kernel,
-        "prepare",
+    weight = call(
+        weight_kernel,
+        "weight",
         [],
-        [
-            shape((queries, cands), jnp.int32),
-            shape((noise_rows, LANES), F32),
-            shape((width, width), BF16),
-            shape((DIGIT * queries, cands), BF16),
-        ],
-        [candidates[0], noise, weight],
-        (pltpu.VMEM((noise_rows, LANES), F32), pltpu.SemaphoreType.DMA((3,))),
+        shape((width, width), BF16),
+        [weight],
+        (pltpu.SemaphoreType.DMA,),
     )
     kept_turned, sent, d_pre = call(
         functools.partial(main_kernel, towers, capacity, fanout),

time: 28.4 us -> 28.4 us (level)
  no operation moved by 1% of the time
where the time goes in v2:
time: 28.4 us; the launch traced here: 28.3 us
  starting transfers between devices  14.3 us (50%)
  waiting for transfers between devices  7.15 us (25%)
  Pallas kernels  6.09 us (21%)
  between operations  0.72 us (3%)
    pallas_call x12, Pallas kernels, call(): pl.pallas_call(kernel, out_shape=out_shape, in_specs=[hbm] * len(from_hbm...  6.09 us
    ppermute x2, starting transfers between devices, swap_near(): lax.ppermute(array, 'z', [(i, i ^ towers // 2) for i in range(towers)])  5.74 us
    ppermute x3, starting transfers between devices, swap_replica(): lax.ppermute(array, 'replica', [(i, i ^ s) for i in range(replicas)])  3.57 us
    ppermute x2, starting transfers between devices, swap_far(): lax.ppermute(array, ('z', 'core'), [(2 * i + c, 2 * (i ^ j + c * towers /...  3.18 us
    ppermute x5, waiting for transfers between devices, swap_core(): return lax.ppermute(array, 'core', [(0, 1), (1, 0)])  3.01 us
    ppermute x3, waiting for transfers between devices, swap_replica(): lax.ppermute(array, 'replica', [(i, i ^ s) for i in range(replicas)])  1.99 us
    ppermute x5, starting transfers between devices, swap_core(): return lax.ppermute(array, 'core', [(0, 1), (1, 0)])  1.81 us
    ppermute x2, waiting for transfers between devices, swap_near(): lax.ppermute(array, 'z', [(i, i ^ towers // 2) for i in range(towers)])  1.22 us
  transfers between devices with their start and end apart: 12, of which 9 were waited for; matrix products, arithmetic and copies ran while one was open for 0% of the time, Pallas kernels for 8%

profile of v2, /device:TPU:0, one launch (start us, length us, event | category | flops | bytes accessed | tf_op | source)
XLA Modules:
  0.0 28.3 jit_solution(8874253229761896008)
XLA Ops:
  0.6 1.1 %outgoing.1 = (f32[8,512]{1,0:T(8,128)S(1)}, f32[8,512]{1,0:T(8,128)S(1)}, bf16[16,128]{1,0:T(8,128)(2,1)S(1)}, f32[16,128]{1,0:T(8,128)S(1)}, bf16[128,512]{1,0...) custom-call(s32[2,8]{1,0:T(2,128)} %bitcast.19, s32[1,8]{1,0:T(1,128)} %bitcast.20, ...), custom_call_target="tpu_custom_call" | custom-call | tf_op jit(solution)/shard_map/outgoing/pallas_call | solution.py:419
  1.8 0.5 %collective-permute-start = (f32[8,512]{1,0:T(8,128)S(1)}, f32[8,512]{1,0:T(8,128)S(1)}, u32[]{:S(2)}, u32[]{:S(2)}) collective-permute-start(f32[8,512]{1,0:T(8,128)S(1)} %get-tuple-element.43), channel_id=1, source_target_pairs={{0,4},{4,0},{1,5},{5,1},{2,6},{6,2},{3,7},{7,3},{8,12},{12,8},{9,1... | collective-permute-start | bytes 49160 | tf_op jit(solution)/shard_map/ppermute | solution.py:430
  2.3 0.4 %prepare.1 = (bf16[128,128]{1,0:T(8,128)(2,1)S(1)}, bf16[16,128]{1,0:T(8,128)(2,1)S(1)}, bf16[128,16]{1,0:T(8,128)(2,1)S(1)}, f32[128,512]{1,0:T(8,128)S(1)}, bf...) custom-call(f32[16,128]{1,0:T(8,128)S(1)} %get-tuple-element.33.held_ref, ...), custom_call_target="tpu_custom_call" | custom-call | tf_op jit(solution)/shard_map/prepare/pallas_call | solution.py:419
  2.7 0.5 %collective-permute-done.arrived_ref.halo_arrived_ref = f32[8,512]{1,0:T(8,128)S(1)} collective-permute-done((f32[8,512]{1,0:T(8,128)S(1)}, f32[8,512]{1,0:T(8,128)S(1)}, u32[]{:S(2)}, u32[]{:S(2)}) %collective-permute-start) | collective-permute-done | bytes 16416 | tf_op jit(solution)/shard_map/ppermute | solution.py:430
  3.1 3.0 %collective-permute-start.1 = (bf16[8,512]{1,0:T(8,128)(2,1)S(1)}, bf16[8,512]{1,0:T(8,128)(2,1)S(1)}, u32[]{:S(2)}, u32[]{:S(2)}) collective-permute-start(bf16[8,512]{1,0:T(8,128)(2,1)S(1)} %get-tuple-element.45), channel_id=1, source_target_pairs={{0,8},{4,28},{8,0},{12,20},{16,24},{20,12},{24,16},{28,4},{1,9},{5... | collective-permute-start | bytes 24584 | tf_op jit(solution)/shard_map/ppermute | solution.py:437
  6.1 2.6 %collective-permute-start.3 = (bf16[4,512]{1,0:T(4,128)(2,1)S(1)}, bf16[4,512]{1,0:T(4,128)(2,1)S(1)}, u32[]{:S(2)}, u32[]{:S(2)}) collective-permute-start(bf16[4,512]{1,0:T(4,128)(2,1)S(1)} %get-tuple-element.46), channel_id=1, source_target_pairs={{0,16},{8,24},{16,0},{24,8},{1,17},{9,25},{17,1},{25,9},{2,18},{10... | collective-permute-start | bytes 12296 | tf_op jit(solution)/shard_map/ppermute | solution.py:433
  8.7 0.4 %collective-permute-start.2 = (bf16[4,512]{1,0:T(4,128)(2,1)S(1)}, bf16[4,512]{1,0:T(4,128)(2,1)S(1)}, u32[]{:S(2)}, u32[]{:S(2)}) collective-permute-start(bf16[4,512]{1,0:T(4,128)(2,1)S(1)} %halo_pass.1), channel_id=1, source_target_pairs={{0,4},{4,0},{1,5},{5,1},{2,6},{6,2},{3,7},{7,3},{8,12},{12,8},{9,1... | collective-permute-start | bytes 12296 | tf_op jit(solution)/shard_map/ppermute | solution.py:430
  9.1 1.0 %weight.1.weight_ref = bf16[512,512]{1,0:T(8,128)(2,1)S(1)} custom-call(bf16[512,512]{1,0:T(8,128)(2,1)} %weight_hbm.1), custom_call_target="tpu_custom_call" | custom-call | tf_op jit(solution)/shard_map/weight/pallas_call | solution.py:419
  10.1 0.5 %collective-permute-done.3.refs_2_ = bf16[4,512]{1,0:T(4,128)(2,1)S(1)} collective-permute-done((bf16[4,512]{1,0:T(4,128)(2,1)S(1)}, bf16[4,512]{1,0:T(4,128)(2,1)S(1)}, u32[]{:S(2)}, u32[]{:S(2)}) %collective-permute-start.3) | collective-permute-done | bytes 4128 | tf_op jit(solution)/shard_map/ppermute | solution.py:433
  10.6 1.8 %forward_backward.1 = (bf16[256,128]{1,0:T(8,128)(2,1)S(1)}, bf16[256,512]{1,0:T(8,128)(2,1)S(1)}, bf16[128,512]{1,0:T(8,128)(2,1)S(1)}) custom-call(bf16[128,16]{1,0:T(8,128)(2,1)S(1)} %get-tuple-element.38.far_turned_ref, f32[128,512]{1,0:T(8,128)S(1)} %get-tuple-element.39.start_ref, s32[32,512]{1,0:T(8,128)S(1)} %get-tuple-element.36.candidates_ref, ...), custom_call_target="tpu_custom_call" | custom-call | tf_op jit(solution)/shard_map/forward_backward/pallas_call | solution.py:419
  12.5 0.8 %collective-permute-start.5 = (bf16[256,512]{1,0:T(8,128)(2,1)S(1)}, bf16[256,512]{1,0:T(8,128)(2,1)S(1)}, u32[]{:S(2)}, u32[]{:S(2)}) collective-permute-start(bf16[256,512]{1,0:T(8,128)(2,1)S(1)} %get-tuple-element.54), channel_id=1, source_target_pairs={{0,4},{4,0},{1,5},{5,1},{2,6},{6,2},{3,7},{7,3},{8,12},{12,8},{9,1... | collective-permute-start | bytes 786440 | tf_op jit(solution)/shard_map/ppermute | solution.py:430
  13.4 1.0 %collective-permute-done.5.arrived_ref = bf16[256,512]{1,0:T(8,128)(2,1)S(1)} collective-permute-done((bf16[256,512]{1,0:T(8,128)(2,1)S(1)}, bf16[256,512]{1,0:T(8,128)(2,1)S(1)}, u32[]{:S(2)}, u32[]{:S(2)}) %collective-permute-start.5) | collective-permute-done | bytes 262176 | tf_op jit(solution)/shard_map/ppermute | solution.py:430
  14.5 2.5 %collective-permute-start.6 = (bf16[256,128]{1,0:T(8,128)(2,1)S(1)}, bf16[256,128]{1,0:T(8,128)(2,1)S(1)}, u32[]{:S(2)}, u32[]{:S(2)}) collective-permute-start(bf16[256,128]{1,0:T(8,128)(2,1)S(1)} %get-tuple-element.56), channel_id=1, source_target_pairs={{0,3},{1,2},{2,1},{3,0},{4,7},{5,6},{6,5},{7,4},{8,11},{9,10},{10,... | collective-permute-start | bytes 196616 | tf_op jit(solution)/shard_map/ppermute | solution.py:447
  17.0 0.5 %collective-permute-start.7 = (bf16[256,128]{1,0:T(8,128)(2,1)S(1)}, bf16[256,128]{1,0:T(8,128)(2,1)S(1)}, u32[]{:S(2)}, u32[]{:S(2)}) collective-permute-start(bf16[256,128]{1,0:T(8,128)(2,1)S(1)} %get-tuple-element.57), channel_id=1, source_target_pairs={{0,2},{1,3},{2,0},{3,1},{4,6},{5,7},{6,4},{7,5},{8,10},{9,11},{10,... | collective-permute-start | bytes 196616 | tf_op jit(solution)/shard_map/ppermute | solution.py:447
  17.5 0.5 %collective-permute-start.8 = (bf16[256,128]{1,0:T(8,128)(2,1)S(1)}, bf16[256,128]{1,0:T(8,128)(2,1)S(1)}, u32[]{:S(2)}, u32[]{:S(2)}) collective-permute-start(bf16[256,128]{1,0:T(8,128)(2,1)S(1)} %get-tuple-element.58), channel_id=1, source_target_pairs={{0,1},{1,0},{2,3},{3,2},{4,5},{5,4},{6,7},{7,6},{8,9},{9,8},{10,11... | collective-permute-start | bytes 196616 | tf_op jit(solution)/shard_map/ppermute | solution.py:447
  18.1 0.5 %spread.1 = (f32[128,512]{1,0:T(8,128)S(1)}, f32[8,512]{1,0:T(8,128)S(1)}, f32[8,512]{1,0:T(8,128)S(1)}) custom-call(bf16[128,512]{1,0:T(8,128)(2,1)S(1)} %get-tuple-element.47.d_pre_ref, bf16[512,512]{1,0:T(8,128)(2,1)S(1)} %weight.1.weight_ref, bf16[128,128]{1,0:T(8,128)(2,1)S(1)} %get-tuple-element.48.own_ref, ...), custom_call_target="tpu_custom_call" | custom-call | tf_op jit(solution)/shard_map/spread/pallas_call | solution.py:419
  18.6 1.2 %collective-permute-done.4.refs_5_.arrived_ref = f32[8,512]{1,0:T(8,128)S(1)} collective-permute-done((f32[8,512]{1,0:T(8,128)S(1)}, f32[8,512]{1,0:T(8,128)S(1)}, u32[]{:S(2)}, u32[]{:S(2)}) %collective-permute-start.4) | collective-permute-done | bytes 16416 | tf_op jit(solution)/shard_map/ppermute | solution.py:430
  19.8 1.4 %collective-permute-done.7.refs_2_ = bf16[256,128]{1,0:T(8,128)(2,1)S(1)} collective-permute-done((bf16[256,128]{1,0:T(8,128)(2,1)S(1)}, bf16[256,128]{1,0:T(8,128)(2,1)S(1)}, u32[]{:S(2)}, u32[]{:S(2)}) %collective-permute-start.7) | collective-permute-done | bytes 65568 | tf_op jit(solution)/shard_map/ppermute | solution.py:447
  21.3 0.5 %collective-permute-done.8.refs_3_ = bf16[256,128]{1,0:T(8,128)(2,1)S(1)} collective-permute-done((bf16[256,128]{1,0:T(8,128)(2,1)S(1)}, bf16[256,128]{1,0:T(8,128)(2,1)S(1)}, u32[]{:S(2)}, u32[]{:S(2)}) %collective-permute-start.8) | collective-permute-done | bytes 65568 | tf_op jit(solution)/shard_map/ppermute | solution.py:447
  22.0 3.2 %collective-permute-start.11 = (bf16[80,128]{1,0:T(8,128)(2,1)S(1)}, bf16[80,128]{1,0:T(8,128)(2,1)S(1)}, u32[]{:S(2)}, u32[]{:S(2)}) collective-permute-start(bf16[80,128]{1,0:T(8,128)(2,1)S(1)} %get-tuple-element.61), channel_id=1, source_target_pairs={{0,16},{8,24},{16,0},{24,8},{1,17},{9,25},{17,1},{25,9},{2,18},{10... | collective-permute-start | bytes 61448 | tf_op jit(solution)/shard_map/ppermute | solution.py:433
  25.2 0.9 %collective-permute-done.9.refs_0_ = bf16[160,128]{1,0:T(8,128)(2,1)S(1)} collective-permute-done((bf16[160,128]{1,0:T(8,128)(2,1)S(1)}, bf16[160,128]{1,0:T(8,128)(2,1)S(1)}, u32[]{:S(2)}, u32[]{:S(2)}) %collective-permute-start.9) | collective-permute-done | bytes 40992 | tf_op jit(solution)/shard_map/ppermute | solution.py:437
  26.2 0.7 %collective-permute-done.11.refs_2_ = bf16[80,128]{1,0:T(8,128)(2,1)S(1)} collective-permute-done((bf16[80,128]{1,0:T(8,128)(2,1)S(1)}, bf16[80,128]{1,0:T(8,128)(2,1)S(1)}, u32[]{:S(2)}, u32[]{:S(2)}) %collective-permute-start.11) | collective-permute-done | bytes 20512 | tf_op jit(solution)/shard_map/ppermute | solution.py:433
  27.0 0.4 %collective-permute-done.10.refs_1_ = bf16[80,128]{1,0:T(8,128)(2,1)S(1)} collective-permute-done((bf16[80,128]{1,0:T(8,128)(2,1)S(1)}, bf16[80,128]{1,0:T(8,128)(2,1)S(1)}, u32[]{:S(2)}, u32[]{:S(2)}) %collective-permute-start.10) | collective-permute-done | bytes 20512 | tf_op jit(solution)/shard_map/ppermute | solution.py:430
  27.4 0.9 %final.1 = (bf16[128,512]{1,0:T(8,128)(2,1)}, f32[64,128]{1,0:T(8,128)}) custom-call(f32[128,512]{1,0:T(8,128)S(1)} %get-tuple-element.49.local_ref, bf16[16,128]{1,0:T(8,128)(2,1)S(1)} %get-tuple-element.50.onehot_ref, f32[8,512]{1,0:T(8,128)S(1)} %get-tuple-element.51.refs_4_.kept_ref, f32[8,512]{1,0:T(8,128)S(1)} %collective-permute-done.4.refs_5_.arrived_ref, ...), custom_call_target="tpu_custom_call" | custom-call | tf_op jit(solution)/shard_map/final/pallas_call | solution.py:419
  (12 shorter events, 0.7 us)
Async XLA Ops:
  1.8 1.4 %collective-permute-start = (f32[8,512]{1,0:T(8,128)S(1)}, f32[8,512]{1,0:T(8,128)S(1)}, u32[]{:S(2)}, u32[]{:S(2)}) collective-permute-start(f32[8,512]{1,0:T(8,128)S(1)} %get-tuple-element.43), channel_id=1, source_target_pairs={{0,4},{4,0},{1,5},{5,1},{2,6},{6,2},{3,7},{7,3},{8,12},{12,8},{9,1... | collective-permute-start | bytes 49160 | tf_op jit(solution)/shard_map/ppermute | solution.py:430
  3.1 5.6 %collective-permute-start.1 = (bf16[8,512]{1,0:T(8,128)(2,1)S(1)}, bf16[8,512]{1,0:T(8,128)(2,1)S(1)}, u32[]{:S(2)}, u32[]{:S(2)}) collective-permute-start(bf16[8,512]{1,0:T(8,128)(2,1)S(1)} %get-tuple-element.45), channel_id=1, source_target_pairs={{0,8},{4,28},{8,0},{12,20},{16,24},{20,12},{24,16},{28,4},{1,9},{5... | collective-permute-start | bytes 24584 | tf_op jit(solution)/shard_map/ppermute | solution.py:437
  6.1 4.5 %collective-permute-start.3 = (bf16[4,512]{1,0:T(4,128)(2,1)S(1)}, bf16[4,512]{1,0:T(4,128)(2,1)S(1)}, u32[]{:S(2)}, u32[]{:S(2)}) collective-permute-start(bf16[4,512]{1,0:T(4,128)(2,1)S(1)} %get-tuple-element.46), channel_id=1, source_target_pairs={{0,16},{8,24},{16,0},{24,8},{1,17},{9,25},{17,1},{25,9},{2,18},{10... | collective-permute-start | bytes 12296 | tf_op jit(solution)/shard_map/ppermute | solution.py:433
  8.7 1.9 %collective-permute-start.2 = (bf16[4,512]{1,0:T(4,128)(2,1)S(1)}, bf16[4,512]{1,0:T(4,128)(2,1)S(1)}, u32[]{:S(2)}, u32[]{:S(2)}) collective-permute-start(bf16[4,512]{1,0:T(4,128)(2,1)S(1)} %halo_pass.1), channel_id=1, source_target_pairs={{0,4},{4,0},{1,5},{5,1},{2,6},{6,2},{3,7},{7,3},{8,12},{12,8},{9,1... | collective-permute-start | bytes 12296 | tf_op jit(solution)/shard_map/ppermute | solution.py:430
  12.5 1.9 %collective-permute-start.5 = (bf16[256,512]{1,0:T(8,128)(2,1)S(1)}, bf16[256,512]{1,0:T(8,128)(2,1)S(1)}, u32[]{:S(2)}, u32[]{:S(2)}) collective-permute-start(bf16[256,512]{1,0:T(8,128)(2,1)S(1)} %get-tuple-element.54), channel_id=1, source_target_pairs={{0,4},{4,0},{1,5},{5,1},{2,6},{6,2},{3,7},{7,3},{8,12},{12,8},{9,1... | collective-permute-start | bytes 786440 | tf_op jit(solution)/shard_map/ppermute | solution.py:430
  14.5 5.3 %collective-permute-start.6 = (bf16[256,128]{1,0:T(8,128)(2,1)S(1)}, bf16[256,128]{1,0:T(8,128)(2,1)S(1)}, u32[]{:S(2)}, u32[]{:S(2)}) collective-permute-start(bf16[256,128]{1,0:T(8,128)(2,1)S(1)} %get-tuple-element.56), channel_id=1, source_target_pairs={{0,3},{1,2},{2,1},{3,0},{4,7},{5,6},{6,5},{7,4},{8,11},{9,10},{10,... | collective-permute-start | bytes 196616 | tf_op jit(solution)/shard_map/ppermute | solution.py:447
  17.0 4.3 %collective-permute-start.7 = (bf16[256,128]{1,0:T(8,128)(2,1)S(1)}, bf16[256,128]{1,0:T(8,128)(2,1)S(1)}, u32[]{:S(2)}, u32[]{:S(2)}) collective-permute-start(bf16[256,128]{1,0:T(8,128)(2,1)S(1)} %get-tuple-element.57), channel_id=1, source_target_pairs={{0,2},{1,3},{2,0},{3,1},{4,6},{5,7},{6,4},{7,5},{8,10},{9,11},{10,... | collective-permute-start | bytes 196616 | tf_op jit(solution)/shard_map/ppermute | solution.py:447
  17.5 4.3 %collective-permute-start.8 = (bf16[256,128]{1,0:T(8,128)(2,1)S(1)}, bf16[256,128]{1,0:T(8,128)(2,1)S(1)}, u32[]{:S(2)}, u32[]{:S(2)}) collective-permute-start(bf16[256,128]{1,0:T(8,128)(2,1)S(1)} %get-tuple-element.58), channel_id=1, source_target_pairs={{0,1},{1,0},{2,3},{3,2},{4,5},{5,4},{6,7},{7,6},{8,9},{9,8},{10,11... | collective-permute-start | bytes 196616 | tf_op jit(solution)/shard_map/ppermute | solution.py:447
  18.6 1.2 %collective-permute-start.4 = (f32[8,512]{1,0:T(8,128)S(1)}, f32[8,512]{1,0:T(8,128)S(1)}, u32[]{:S(2)}, u32[]{:S(2)}) collective-permute-start(f32[8,512]{1,0:T(8,128)S(1)} %get-tuple-element.52), channel_id=1, source_target_pairs={{0,4},{4,0},{1,5},{5,1},{2,6},{6,2},{3,7},{7,3},{8,12},{12,8},{9,1... | collective-permute-start | bytes 49160 | tf_op jit(solution)/shard_map/ppermute | solution.py:430
  21.8 4.3 %collective-permute-start.9 = (bf16[160,128]{1,0:T(8,128)(2,1)S(1)}, bf16[160,128]{1,0:T(8,128)(2,1)S(1)}, u32[]{:S(2)}, u32[]{:S(2)}) collective-permute-start(bf16[160,128]{1,0:T(8,128)(2,1)S(1)} %get-tuple-element.60), channel_id=1, source_target_pairs={{0,8},{4,28},{8,0},{12,20},{16,24},{20,12},{24,16},{28,4},{1,9},{5... | collective-permute-start | bytes 122888 | tf_op jit(solution)/shard_map/ppermute | solution.py:437
  22.0 4.9 %collective-permute-start.11 = (bf16[80,128]{1,0:T(8,128)(2,1)S(1)}, bf16[80,128]{1,0:T(8,128)(2,1)S(1)}, u32[]{:S(2)}, u32[]{:S(2)}) collective-permute-start(bf16[80,128]{1,0:T(8,128)(2,1)S(1)} %get-tuple-element.61), channel_id=1, source_target_pairs={{0,16},{8,24},{16,0},{24,8},{1,17},{9,25},{17,1},{25,9},{2,18},{10... | collective-permute-start | bytes 61448 | tf_op jit(solution)/shard_map/ppermute | solution.py:433
  26.1 1.3 %collective-permute-start.10 = (bf16[80,128]{1,0:T(8,128)(2,1)S(1)}, bf16[80,128]{1,0:T(8,128)(2,1)S(1)}, u32[]{:S(2)}, u32[]{:S(2)}) collective-permute-start(bf16[80,128]{1,0:T(8,128)(2,1)S(1)} %pass_sums.1), channel_id=1, source_target_pairs={{0,4},{4,0},{1,5},{5,1},{2,6},{6,2},{3,7},{7,3},{8,12},{12,8},{9,1... | collective-permute-start | bytes 61448 | tf_op jit(solution)/shard_map/ppermute | solution.py:430

commit v3 on v1

--- a/solution.py
+++ b/solution.py
@@ -269,9 +269,10 @@
     embedded = (pre * inverse).astype(BF16)
     factor = SCORE_SCALE / width
     rounded = pre.astype(BF16)
-    similar = dot(rounded[:queries], rounded, NT)
-    inverse_of_column = jnp.broadcast_to(inverse, (rows, rows)).T[:queries]
-    similar = similar * (factor * inverse[:queries] * inverse_of_column)
+    products = dot(rounded[:queries], rounded, NT)
+    turned_products = dot(rounded, rounded[:queries], NT)
+    inverse_of_column = jnp.broadcast_to(inverse, (rows, rows)).T
+    similar = products * (factor * inverse[:queries] * inverse_of_column[:queries])
     blocks = cands // LANES
     scores = [
         jnp.take_along_axis(similar, candidates_ref[:, j * LANES : (j + 1) * LANES], axis=1)
@@ -310,7 +311,12 @@
     d_embedded = jnp.concatenate(
         [d_embedded[:queries] + d_queries, d_embedded[queries:]], axis=0
     )
-    inner = jnp.mean(d_embedded * pre, axis=-1, keepdims=True)
+    wide = d_similar.astype(F32)
+    inner = jnp.sum(wide * turned_products * inverse_of_column[:, :queries], axis=-1, keepdims=True)
+    inner_queries = jnp.sum(wide.T * products * inverse_of_column[:queries], axis=-1, keepdims=True)
+    inner = (factor / width) * jnp.concatenate(
+        [inner[:queries] + inner_queries, inner[queries:]], axis=0
+    )
     d_pre = (inverse * d_embedded - inverse * inverse * inverse * pre * inner).astype(BF16)
 
     d_pre_ref[...] = d_pre

time: 28.4 us -> 28.4 us (level)
  no operation moved by 1% of the time
where the time goes in v3:
time: 28.4 us; the launch traced here: 28.2 us
  starting transfers between devices  14.4 us (51%)
  waiting for transfers between devices  6.96 us (25%)
  Pallas kernels  6.11 us (22%)
  between operations  0.72 us (3%)
    pallas_call x12, Pallas kernels, call(): pl.pallas_call(kernel, out_shape=out_shape, in_specs=[hbm] * len(from_hbm...  6.11 us
    ppermute x2, starting transfers between devices, swap_near(): lax.ppermute(array, 'z', [(i, i ^ towers // 2) for i in range(towers)])  5.8 us
    ppermute x3, starting transfers between devices, swap_replica(): lax.ppermute(array, 'replica', [(i, i ^ s) for i in range(replicas)])  3.57 us
    ppermute x2, starting transfers between devices, swap_far(): lax.ppermute(array, ('z', 'core'), [(2 * i + c, 2 * (i ^ j + c * towers /...  3.27 us
    ppermute x5, waiting for transfers between devices, swap_core(): return lax.ppermute(array, 'core', [(0, 1), (1, 0)])  2.96 us
    ppermute x3, waiting for transfers between devices, swap_replica(): lax.ppermute(array, 'replica', [(i, i ^ s) for i in range(replicas)])  1.99 us
    ppermute x5, starting transfers between devices, swap_core(): return lax.ppermute(array, 'core', [(0, 1), (1, 0)])  1.81 us
    ppermute x2, waiting for transfers between devices, swap_near(): lax.ppermute(array, 'z', [(i, i ^ towers // 2) for i in range(towers)])  1.22 us
  transfers between devices with their start and end apart: 12, of which 9 were waited for; matrix products, arithmetic and copies ran while one was open for 0% of the time, Pallas kernels for 8%

profile of v3, /device:TPU:0, one launch (start us, length us, event | category | flops | bytes accessed | tf_op | source)
XLA Modules:
  0.0 28.2 jit_solution(8192485187853722741)
XLA Ops:
  0.6 1.1 %outgoing.1 = (f32[8,512]{1,0:T(8,128)S(1)}, f32[8,512]{1,0:T(8,128)S(1)}, bf16[16,128]{1,0:T(8,128)(2,1)S(1)}, f32[16,128]{1,0:T(8,128)S(1)}, bf16[128,512]{1,0:T(8,128)(2,1)S(1)}, /*index=5*/s32[16,128]{1,0:T(8,128)S(1)}) custom-call(s32[2,8]{1,0:T(2,128)} %bitcast.19, s32[1,8]{1,0:T(1,128)} %bitcast.20, bf16[128,512]{1,0:T(8,128)(2,1)} %bitcast.16, ...), custom_call_target="tpu_custom_call" | custom-call | tf_op jit(solution)/shard_map/outgoing/pallas_call | solution.py:427
  1.7 0.5 %collective-permute-start = (f32[8,512]{1,0:T(8,128)S(1)}, f32[8,512]{1,0:T(8,128)S(1)}, u32[]{:S(2)}, u32[]{:S(2)}) collective-permute-start(f32[8,512]{1,0:T(8,128)S(1)} %get-tuple-element.43), channel_id=1, source_target_pairs={{0,4},{4,0},{1,5},{5,1},{2,6},{6,2},{3,7},{7,3},{8,12},{12,8},{9,1... | collective-permute-start | bytes 49160 | tf_op jit(solution)/shard_map/ppermute | solution.py:438
  2.2 0.3 %adjacency.1 = (bf16[128,128]{1,0:T(8,128)(2,1)S(1)}, bf16[16,128]{1,0:T(8,128)(2,1)S(1)}, bf16[128,16]{1,0:T(8,128)(2,1)S(1)}, f32[128,512]{1,0:T(8,128)S(1)}) custom-call(f32[16,128]{1,0:T(8,128)S(1)} %get-tuple-element.33.held_ref, bf16[128,512]{1,0:T(8,128)(2,1)S(1)} %get-tuple-element.34.features_ref, s32[16,128]{1,0:T(8,128)S(1)} %get-tuple-element.35.neighbours_ref), custom_call_target="tpu_custom_call" | custom-call | tf_op jit(solution)/shard_map/adjacency/pallas_call | solution.py:427
  2.5 0.5 %collective-permute-done.arrived_ref.halo_arrived_ref = f32[8,512]{1,0:T(8,128)S(1)} collective-permute-done((f32[8,512]{1,0:T(8,128)S(1)}, f32[8,512]{1,0:T(8,128)S(1)}, u32[]{:S(2)}, u32[]{:S(2)}) %collective-permute-start) | collective-permute-done | bytes 16416 | tf_op jit(solution)/shard_map/ppermute | solution.py:438
  3.1 3.0 %collective-permute-start.1 = (bf16[8,512]{1,0:T(8,128)(2,1)S(1)}, bf16[8,512]{1,0:T(8,128)(2,1)S(1)}, u32[]{:S(2)}, u32[]{:S(2)}) collective-permute-start(bf16[8,512]{1,0:T(8,128)(2,1)S(1)} %get-tuple-element.45), channel_id=1, source_target_pairs={{0,8},{4,28},{8,0},{12,20},{16,24},{20,12},{24,16},{28,4},{1,9},{5... | collective-permute-start | bytes 24584 | tf_op jit(solution)/shard_map/ppermute | solution.py:445
  6.1 2.6 %collective-permute-start.3 = (bf16[4,512]{1,0:T(4,128)(2,1)S(1)}, bf16[4,512]{1,0:T(4,128)(2,1)S(1)}, u32[]{:S(2)}, u32[]{:S(2)}) collective-permute-start(bf16[4,512]{1,0:T(4,128)(2,1)S(1)} %get-tuple-element.46), channel_id=1, source_target_pairs={{0,16},{8,24},{16,0},{24,8},{1,17},{9,25},{17,1},{25,9},{2,18},{10... | collective-permute-start | bytes 12296 | tf_op jit(solution)/shard_map/ppermute | solution.py:441
  8.7 0.4 %collective-permute-start.2 = (bf16[4,512]{1,0:T(4,128)(2,1)S(1)}, bf16[4,512]{1,0:T(4,128)(2,1)S(1)}, u32[]{:S(2)}, u32[]{:S(2)}) collective-permute-start(bf16[4,512]{1,0:T(4,128)(2,1)S(1)} %halo_pass.1), channel_id=1, source_target_pairs={{0,4},{4,0},{1,5},{5,1},{2,6},{6,2},{3,7},{7,3},{8,12},{12,8},{9,1... | collective-permute-start | bytes 12296 | tf_op jit(solution)/shard_map/ppermute | solution.py:438
  9.0 1.2 %prepare.1 = (s32[32,512]{1,0:T(8,128)S(1)}, f32[512,128]{1,0:T(8,128)S(1)}, bf16[512,512]{1,0:T(8,128)(2,1)S(1)}, bf16[512,512]{1,0:T(8,128)(2,1)S(1)}) custom-call(s32[32,512]{1,0:T(8,128)} %bitcast.17, f32[512,128]{1,0:T(8,128)} %bitcast.15, bf16[512,512]{1,0:T(8,128)(2,1)} %weight_hbm.1), custom_call_target="tpu_custom_call" | custom-call | tf_op jit(solution)/shard_map/prepare/pallas_call | solution.py:427
  10.2 0.3 %collective-permute-done.3.refs_2_ = bf16[4,512]{1,0:T(4,128)(2,1)S(1)} collective-permute-done((bf16[4,512]{1,0:T(4,128)(2,1)S(1)}, bf16[4,512]{1,0:T(4,128)(2,1)S(1)}, u32[]{:S(2)}, u32[]{:S(2)}) %collective-permute-start.3) | collective-permute-done | bytes 4128 | tf_op jit(solution)/shard_map/ppermute | solution.py:441
  10.6 1.8 %forward_backward.1 = (bf16[256,128]{1,0:T(8,128)(2,1)S(1)}, bf16[256,512]{1,0:T(8,128)(2,1)S(1)}, bf16[128,512]{1,0:T(8,128)(2,1)S(1)}) custom-call(bf16[128,16]{1,0:T(8,128)(2,1)S(1)} %get-tuple-element.36.far_turned_ref, f32[128,512]{1,0:T(8,128)S(1)} %get-tuple-element.37.start_ref, s32[32,512]{1,0:T(8,128)S(1)} %get-tuple-element.38.candidates_ref, ...), custom_call_target="tpu_custom_call" | custom-call | tf_op jit(solution)/shard_map/forward_backward/pallas_call | solution.py:427
  12.4 0.8 %collective-permute-start.5 = (bf16[256,512]{1,0:T(8,128)(2,1)S(1)}, bf16[256,512]{1,0:T(8,128)(2,1)S(1)}, u32[]{:S(2)}, u32[]{:S(2)}) collective-permute-start(bf16[256,512]{1,0:T(8,128)(2,1)S(1)} %get-tuple-element.54), channel_id=1, source_target_pairs={{0,4},{4,0},{1,5},{5,1},{2,6},{6,2},{3,7},{7,3},{8,12},{12,8},{9,1... | collective-permute-start | bytes 786440 | tf_op jit(solution)/shard_map/ppermute | solution.py:438
  13.4 1.0 %collective-permute-done.5.arrived_ref = bf16[256,512]{1,0:T(8,128)(2,1)S(1)} collective-permute-done((bf16[256,512]{1,0:T(8,128)(2,1)S(1)}, bf16[256,512]{1,0:T(8,128)(2,1)S(1)}, u32[]{:S(2)}, u32[]{:S(2)}) %collective-permute-start.5) | collective-permute-done | bytes 262176 | tf_op jit(solution)/shard_map/ppermute | solution.py:438
  14.5 2.5 %collective-permute-start.6 = (bf16[256,128]{1,0:T(8,128)(2,1)S(1)}, bf16[256,128]{1,0:T(8,128)(2,1)S(1)}, u32[]{:S(2)}, u32[]{:S(2)}) collective-permute-start(bf16[256,128]{1,0:T(8,128)(2,1)S(1)} %get-tuple-element.56), channel_id=1, source_target_pairs={{0,3},{1,2},{2,1},{3,0},{4,7},{5,6},{6,5},{7,4},{8,11},{9,10},{10,... | collective-permute-start | bytes 196616 | tf_op jit(solution)/shard_map/ppermute | solution.py:455
  17.0 0.5 %collective-permute-start.7 = (bf16[256,128]{1,0:T(8,128)(2,1)S(1)}, bf16[256,128]{1,0:T(8,128)(2,1)S(1)}, u32[]{:S(2)}, u32[]{:S(2)}) collective-permute-start(bf16[256,128]{1,0:T(8,128)(2,1)S(1)} %get-tuple-element.57), channel_id=1, source_target_pairs={{0,2},{1,3},{2,0},{3,1},{4,6},{5,7},{6,4},{7,5},{8,10},{9,11},{10,... | collective-permute-start | bytes 196616 | tf_op jit(solution)/shard_map/ppermute | solution.py:455
  17.5 0.5 %collective-permute-start.8 = (bf16[256,128]{1,0:T(8,128)(2,1)S(1)}, bf16[256,128]{1,0:T(8,128)(2,1)S(1)}, u32[]{:S(2)}, u32[]{:S(2)}) collective-permute-start(bf16[256,128]{1,0:T(8,128)(2,1)S(1)} %get-tuple-element.58), channel_id=1, source_target_pairs={{0,1},{1,0},{2,3},{3,2},{4,5},{5,4},{6,7},{7,6},{8,9},{9,8},{10,11... | collective-permute-start | bytes 196616 | tf_op jit(solution)/shard_map/ppermute | solution.py:455
  18.0 0.5 %spread.1 = (f32[128,512]{1,0:T(8,128)S(1)}, f32[8,512]{1,0:T(8,128)S(1)}, f32[8,512]{1,0:T(8,128)S(1)}) custom-call(bf16[128,512]{1,0:T(8,128)(2,1)S(1)} %get-tuple-element.47.d_pre_ref, bf16[512,512]{1,0:T(8,128)(2,1)S(1)} %get-tuple-element.40.weight_ref, bf16[128,128]{1,0:T(8,128)(2,1)S(1)} %get-tuple-element.48.own_ref, ...), custom_call_target="tpu_custom_call" | custom-call | tf_op jit(solution)/shard_map/spread/pallas_call | solution.py:427
  18.6 1.2 %collective-permute-done.4.refs_5_.arrived_ref = f32[8,512]{1,0:T(8,128)S(1)} collective-permute-done((f32[8,512]{1,0:T(8,128)S(1)}, f32[8,512]{1,0:T(8,128)S(1)}, u32[]{:S(2)}, u32[]{:S(2)}) %collective-permute-start.4) | collective-permute-done | bytes 16416 | tf_op jit(solution)/shard_map/ppermute | solution.py:438
  19.8 1.4 %collective-permute-done.7.refs_2_ = bf16[256,128]{1,0:T(8,128)(2,1)S(1)} collective-permute-done((bf16[256,128]{1,0:T(8,128)(2,1)S(1)}, bf16[256,128]{1,0:T(8,128)(2,1)S(1)}, u32[]{:S(2)}, u32[]{:S(2)}) %collective-permute-start.7) | collective-permute-done | bytes 65568 | tf_op jit(solution)/shard_map/ppermute | solution.py:455
  21.3 0.5 %collective-permute-done.8.refs_3_ = bf16[256,128]{1,0:T(8,128)(2,1)S(1)} collective-permute-done((bf16[256,128]{1,0:T(8,128)(2,1)S(1)}, bf16[256,128]{1,0:T(8,128)(2,1)S(1)}, u32[]{:S(2)}, u32[]{:S(2)}) %collective-permute-start.8) | collective-permute-done | bytes 65568 | tf_op jit(solution)/shard_map/ppermute | solution.py:455
  22.1 3.2 %collective-permute-start.11 = (bf16[80,128]{1,0:T(8,128)(2,1)S(1)}, bf16[80,128]{1,0:T(8,128)(2,1)S(1)}, u32[]{:S(2)}, u32[]{:S(2)}) collective-permute-start(bf16[80,128]{1,0:T(8,128)(2,1)S(1)} %get-tuple-element.61), channel_id=1, source_target_pairs={{0,16},{8,24},{16,0},{24,8},{1,17},{9,25},{17,1},{25,9},{2,18},{10... | collective-permute-start | bytes 61448 | tf_op jit(solution)/shard_map/ppermute | solution.py:441
  25.3 0.8 %collective-permute-done.9.refs_0_ = bf16[160,128]{1,0:T(8,128)(2,1)S(1)} collective-permute-done((bf16[160,128]{1,0:T(8,128)(2,1)S(1)}, bf16[160,128]{1,0:T(8,128)(2,1)S(1)}, u32[]{:S(2)}, u32[]{:S(2)}) %collective-permute-start.9) | collective-permute-done | bytes 40992 | tf_op jit(solution)/shard_map/ppermute | solution.py:445
  26.2 0.9 %collective-permute-done.11.refs_2_ = bf16[80,128]{1,0:T(8,128)(2,1)S(1)} collective-permute-done((bf16[80,128]{1,0:T(8,128)(2,1)S(1)}, bf16[80,128]{1,0:T(8,128)(2,1)S(1)}, u32[]{:S(2)}, u32[]{:S(2)}) %collective-permute-start.11) | collective-permute-done | bytes 20512 | tf_op jit(solution)/shard_map/ppermute | solution.py:441
  27.1 0.3 %collective-permute-done.10.refs_1_ = bf16[80,128]{1,0:T(8,128)(2,1)S(1)} collective-permute-done((bf16[80,128]{1,0:T(8,128)(2,1)S(1)}, bf16[80,128]{1,0:T(8,128)(2,1)S(1)}, u32[]{:S(2)}, u32[]{:S(2)}) %collective-permute-start.10) | collective-permute-done | bytes 20512 | tf_op jit(solution)/shard_map/ppermute | solution.py:438
  27.4 0.9 %final.1 = (bf16[128,512]{1,0:T(8,128)(2,1)}, f32[64,128]{1,0:T(8,128)}) custom-call(f32[128,512]{1,0:T(8,128)S(1)} %get-tuple-element.49.local_ref, bf16[16,128]{1,0:T(8,128)(2,1)S(1)} %get-tuple-element.50.onehot_ref, f32[8,512]{1,0:T(8,128)S(1)} %get-tuple-element.51.refs_4_.kept_ref, f32[8,512]{1,0:T(8,128)S(1)} %collective-permute-done.4.refs_5_.arrived_ref, ...), custom_call_target="tpu_custom_call" | custom-call | tf_op jit(solution)/shard_map/final/pallas_call | solution.py:427
  (12 shorter events, 0.8 us)
Async XLA Ops:
  1.7 1.4 %collective-permute-start = (f32[8,512]{1,0:T(8,128)S(1)}, f32[8,512]{1,0:T(8,128)S(1)}, u32[]{:S(2)}, u32[]{:S(2)}) collective-permute-start(f32[8,512]{1,0:T(8,128)S(1)} %get-tuple-element.43), channel_id=1, source_target_pairs={{0,4},{4,0},{1,5},{5,1},{2,6},{6,2},{3,7},{7,3},{8,12},{12,8},{9,1... | collective-permute-start | bytes 49160 | tf_op jit(solution)/shard_map/ppermute | solution.py:438
  3.1 5.6 %collective-permute-start.1 = (bf16[8,512]{1,0:T(8,128)(2,1)S(1)}, bf16[8,512]{1,0:T(8,128)(2,1)S(1)}, u32[]{:S(2)}, u32[]{:S(2)}) collective-permute-start(bf16[8,512]{1,0:T(8,128)(2,1)S(1)} %get-tuple-element.45), channel_id=1, source_target_pairs={{0,8},{4,28},{8,0},{12,20},{16,24},{20,12},{24,16},{28,4},{1,9},{5... | collective-permute-start | bytes 24584 | tf_op jit(solution)/shard_map/ppermute | solution.py:445
  6.1 4.5 %collective-permute-start.3 = (bf16[4,512]{1,0:T(4,128)(2,1)S(1)}, bf16[4,512]{1,0:T(4,128)(2,1)S(1)}, u32[]{:S(2)}, u32[]{:S(2)}) collective-permute-start(bf16[4,512]{1,0:T(4,128)(2,1)S(1)} %get-tuple-element.46), channel_id=1, source_target_pairs={{0,16},{8,24},{16,0},{24,8},{1,17},{9,25},{17,1},{25,9},{2,18},{10... | collective-permute-start | bytes 12296 | tf_op jit(solution)/shard_map/ppermute | solution.py:441
  8.7 1.9 %collective-permute-start.2 = (bf16[4,512]{1,0:T(4,128)(2,1)S(1)}, bf16[4,512]{1,0:T(4,128)(2,1)S(1)}, u32[]{:S(2)}, u32[]{:S(2)}) collective-permute-start(bf16[4,512]{1,0:T(4,128)(2,1)S(1)} %halo_pass.1), channel_id=1, source_target_pairs={{0,4},{4,0},{1,5},{5,1},{2,6},{6,2},{3,7},{7,3},{8,12},{12,8},{9,1... | collective-permute-start | bytes 12296 | tf_op jit(solution)/shard_map/ppermute | solution.py:438
  12.4 1.9 %collective-permute-start.5 = (bf16[256,512]{1,0:T(8,128)(2,1)S(1)}, bf16[256,512]{1,0:T(8,128)(2,1)S(1)}, u32[]{:S(2)}, u32[]{:S(2)}) collective-permute-start(bf16[256,512]{1,0:T(8,128)(2,1)S(1)} %get-tuple-element.54), channel_id=1, source_target_pairs={{0,4},{4,0},{1,5},{5,1},{2,6},{6,2},{3,7},{7,3},{8,12},{12,8},{9,1... | collective-permute-start | bytes 786440 | tf_op jit(solution)/shard_map/ppermute | solution.py:438
  14.5 5.3 %collective-permute-start.6 = (bf16[256,128]{1,0:T(8,128)(2,1)S(1)}, bf16[256,128]{1,0:T(8,128)(2,1)S(1)}, u32[]{:S(2)}, u32[]{:S(2)}) collective-permute-start(bf16[256,128]{1,0:T(8,128)(2,1)S(1)} %get-tuple-element.56), channel_id=1, source_target_pairs={{0,3},{1,2},{2,1},{3,0},{4,7},{5,6},{6,5},{7,4},{8,11},{9,10},{10,... | collective-permute-start | bytes 196616 | tf_op jit(solution)/shard_map/ppermute | solution.py:455
  17.0 4.3 %collective-permute-start.7 = (bf16[256,128]{1,0:T(8,128)(2,1)S(1)}, bf16[256,128]{1,0:T(8,128)(2,1)S(1)}, u32[]{:S(2)}, u32[]{:S(2)}) collective-permute-start(bf16[256,128]{1,0:T(8,128)(2,1)S(1)} %get-tuple-element.57), channel_id=1, source_target_pairs={{0,2},{1,3},{2,0},{3,1},{4,6},{5,7},{6,4},{7,5},{8,10},{9,11},{10,... | collective-permute-start | bytes 196616 | tf_op jit(solution)/shard_map/ppermute | solution.py:455
  17.5 4.3 %collective-permute-start.8 = (bf16[256,128]{1,0:T(8,128)(2,1)S(1)}, bf16[256,128]{1,0:T(8,128)(2,1)S(1)}, u32[]{:S(2)}, u32[]{:S(2)}) collective-permute-start(bf16[256,128]{1,0:T(8,128)(2,1)S(1)} %get-tuple-element.58), channel_id=1, source_target_pairs={{0,1},{1,0},{2,3},{3,2},{4,5},{5,4},{6,7},{7,6},{8,9},{9,8},{10,11... | collective-permute-start | bytes 196616 | tf_op jit(solution)/shard_map/ppermute | solution.py:455
  18.5 1.2 %collective-permute-start.4 = (f32[8,512]{1,0:T(8,128)S(1)}, f32[8,512]{1,0:T(8,128)S(1)}, u32[]{:S(2)}, u32[]{:S(2)}) collective-permute-start(f32[8,512]{1,0:T(8,128)S(1)} %get-tuple-element.52), channel_id=1, source_target_pairs={{0,4},{4,0},{1,5},{5,1},{2,6},{6,2},{3,7},{7,3},{8,12},{12,8},{9,1... | collective-permute-start | bytes 49160 | tf_op jit(solution)/shard_map/ppermute | solution.py:438
  21.8 4.3 %collective-permute-start.9 = (bf16[160,128]{1,0:T(8,128)(2,1)S(1)}, bf16[160,128]{1,0:T(8,128)(2,1)S(1)}, u32[]{:S(2)}, u32[]{:S(2)}) collective-permute-start(bf16[160,128]{1,0:T(8,128)(2,1)S(1)} %get-tuple-element.60), channel_id=1, source_target_pairs={{0,8},{4,28},{8,0},{12,20},{16,24},{20,12},{24,16},{28,4},{1,9},{5... | collective-permute-start | bytes 122888 | tf_op jit(solution)/shard_map/ppermute | solution.py:445
  22.1 5.0 %collective-permute-start.11 = (bf16[80,128]{1,0:T(8,128)(2,1)S(1)}, bf16[80,128]{1,0:T(8,128)(2,1)S(1)}, u32[]{:S(2)}, u32[]{:S(2)}) collective-permute-start(bf16[80,128]{1,0:T(8,128)(2,1)S(1)} %get-tuple-element.61), channel_id=1, source_target_pairs={{0,16},{8,24},{16,0},{24,8},{1,17},{9,25},{17,1},{25,9},{2,18},{10... | collective-permute-start | bytes 61448 | tf_op jit(solution)/shard_map/ppermute | solution.py:441
  26.1 1.3 %collective-permute-start.10 = (bf16[80,128]{1,0:T(8,128)(2,1)S(1)}, bf16[80,128]{1,0:T(8,128)(2,1)S(1)}, u32[]{:S(2)}, u32[]{:S(2)}) collective-permute-start(bf16[80,128]{1,0:T(8,128)(2,1)S(1)} %pass_sums.1), channel_id=1, source_target_pairs={{0,4},{4,0},{1,5},{5,1},{2,6},{6,2},{3,7},{7,3},{8,12},{12,8},{9,1... | collective-permute-start | bytes 61448 | tf_op jit(solution)/shard_map/ppermute | solution.py:438

commit v4 on v1

--- a/solution.py
+++ b/solution.py
@@ -208,18 +208,12 @@
     sems,
 ):
     copies = start_copies(
-        [(candidates_hbm, candidates_ref), (noise_hbm, raw_noise_ref), (weight_hbm, weight_ref)], sems
+        [(noise_hbm, raw_noise_ref), (weight_hbm, weight_ref), (candidates_hbm, candidates_ref)], sems
     )
     queries, cands = candidates_ref.shape
     blocks = cands // LANES
     samples = noise_ref.shape[0] // (queries * blocks)
     copies[0].wait()
-    low = lax.bitwise_and(candidates_ref[...], jnp.int32(DIGIT - 1))
-    for digit in range(DIGIT):
-        marks_ref[digit * queries : (digit + 1) * queries, :] = (
-            (low == digit).astype(F32).astype(BF16)
-        )
-    copies[1].wait()
     for m in range(samples):
         noise = [
             raw_noise_ref[pl.ds(j * samples + m, queries, stride=blocks * samples), :]
@@ -230,6 +224,12 @@
             at = (m * blocks + j) * queries
             noise_ref[at : at + queries, :] = jnp.exp(noise[j] - highest)
     copies[2].wait()
+    low = lax.bitwise_and(candidates_ref[...], jnp.int32(DIGIT - 1))
+    for digit in range(DIGIT):
+        marks_ref[digit * queries : (digit + 1) * queries, :] = (
+            (low == digit).astype(F32).astype(BF16)
+        )
+    copies[1].wait()
 
 
 def main_kernel(

time: 28.4 us -> 28.4 us (level)
  no operation moved by 1% of the time
where the time goes in v4:
time: 28.4 us; the launch traced here: 28.2 us
  starting transfers between devices  14.5 us (51%)
  waiting for transfers between devices  6.88 us (24%)
  Pallas kernels  6.13 us (22%)
  between operations  0.72 us (3%)
    pallas_call x12, Pallas kernels, call(): pl.pallas_call(kernel, out_shape=out_shape, in_specs=[hbm] * len(from_hbm...  6.13 us
    ppermute x2, starting transfers between devices, swap_near(): lax.ppermute(array, 'z', [(i, i ^ towers // 2) for i in range(towers)])  5.8 us
    ppermute x3, starting transfers between devices, swap_replica(): lax.ppermute(array, 'replica', [(i, i ^ s) for i in range(replicas)])  3.57 us
    ppermute x2, starting transfers between devices, swap_far(): lax.ppermute(array, ('z', 'core'), [(2 * i + c, 2 * (i ^ j + c * towers /...  3.31 us
    ppermute x5, waiting for transfers between devices, swap_core(): return lax.ppermute(array, 'core', [(0, 1), (1, 0)])  2.91 us
    ppermute x3, waiting for transfers between devices, swap_replica(): lax.ppermute(array, 'replica', [(i, i ^ s) for i in range(replicas)])  1.99 us
    ppermute x5, starting transfers between devices, swap_core(): return lax.ppermute(array, 'core', [(0, 1), (1, 0)])  1.81 us
    ppermute x2, waiting for transfers between devices, swap_near(): lax.ppermute(array, 'z', [(i, i ^ towers // 2) for i in range(towers)])  1.22 us
  transfers between devices with their start and end apart: 12, of which 9 were waited for; matrix products, arithmetic and copies ran while one was open for 0% of the time, Pallas kernels for 8%

profile of v4, /device:TPU:0, one launch (start us, length us, event | category | flops | bytes accessed | tf_op | source)
XLA Modules:
  0.0 28.2 jit_solution(1453086751112602086)
XLA Ops:
  0.6 1.1 %outgoing.1 = (f32[8,512]{1,0:T(8,128)S(1)}, f32[8,512]{1,0:T(8,128)S(1)}, bf16[16,128]{1,0:T(8,128)(2,1)S(1)}, f32[16,128]{1,0:T(8,128)S(1)}, bf16[128,512]{1,0:T(8,128)(2,1)S(1)}, /*index=5*/s32[16,128]{1,0:T(8,128)S(1)}) custom-call(s32[2,8]{1,0:T(2,128)} %bitcast.19, s32[1,8]{1,0:T(1,128)} %bitcast.20, bf16[128,512]{1,0:T(8,128)(2,1)} %bitcast.16, ...), custom_call_target="tpu_custom_call" | custom-call | tf_op jit(solution)/shard_map/outgoing/pallas_call | solution.py:421
  1.7 0.5 %collective-permute-start = (f32[8,512]{1,0:T(8,128)S(1)}, f32[8,512]{1,0:T(8,128)S(1)}, u32[]{:S(2)}, u32[]{:S(2)}) collective-permute-start(f32[8,512]{1,0:T(8,128)S(1)} %get-tuple-element.43), channel_id=1, source_target_pairs={{0,4},{4,0},{1,5},{5,1},{2,6},{6,2},{3,7},{7,3},{8,12},{12,8},{9,1... | collective-permute-start | bytes 49160 | tf_op jit(solution)/shard_map/ppermute | solution.py:432
  2.2 0.3 %adjacency.1 = (bf16[128,128]{1,0:T(8,128)(2,1)S(1)}, bf16[16,128]{1,0:T(8,128)(2,1)S(1)}, bf16[128,16]{1,0:T(8,128)(2,1)S(1)}, f32[128,512]{1,0:T(8,128)S(1)}) custom-call(f32[16,128]{1,0:T(8,128)S(1)} %get-tuple-element.33.held_ref, bf16[128,512]{1,0:T(8,128)(2,1)S(1)} %get-tuple-element.34.features_ref, s32[16,128]{1,0:T(8,128)S(1)} %get-tuple-element.35.neighbours_ref), custom_call_target="tpu_custom_call" | custom-call | tf_op jit(solution)/shard_map/adjacency/pallas_call | solution.py:421
  2.5 0.5 %collective-permute-done.arrived_ref.halo_arrived_ref = f32[8,512]{1,0:T(8,128)S(1)} collective-permute-done((f32[8,512]{1,0:T(8,128)S(1)}, f32[8,512]{1,0:T(8,128)S(1)}, u32[]{:S(2)}, u32[]{:S(2)}) %collective-permute-start) | collective-permute-done | bytes 16416 | tf_op jit(solution)/shard_map/ppermute | solution.py:432
  3.1 3.0 %collective-permute-start.1 = (bf16[8,512]{1,0:T(8,128)(2,1)S(1)}, bf16[8,512]{1,0:T(8,128)(2,1)S(1)}, u32[]{:S(2)}, u32[]{:S(2)}) collective-permute-start(bf16[8,512]{1,0:T(8,128)(2,1)S(1)} %get-tuple-element.45), channel_id=1, source_target_pairs={{0,8},{4,28},{8,0},{12,20},{16,24},{20,12},{24,16},{28,4},{1,9},{5... | collective-permute-start | bytes 24584 | tf_op jit(solution)/shard_map/ppermute | solution.py:439
  6.1 2.6 %collective-permute-start.3 = (bf16[4,512]{1,0:T(4,128)(2,1)S(1)}, bf16[4,512]{1,0:T(4,128)(2,1)S(1)}, u32[]{:S(2)}, u32[]{:S(2)}) collective-permute-start(bf16[4,512]{1,0:T(4,128)(2,1)S(1)} %get-tuple-element.46), channel_id=1, source_target_pairs={{0,16},{8,24},{16,0},{24,8},{1,17},{9,25},{17,1},{25,9},{2,18},{10... | collective-permute-start | bytes 12296 | tf_op jit(solution)/shard_map/ppermute | solution.py:435
  8.7 0.4 %collective-permute-start.2 = (bf16[4,512]{1,0:T(4,128)(2,1)S(1)}, bf16[4,512]{1,0:T(4,128)(2,1)S(1)}, u32[]{:S(2)}, u32[]{:S(2)}) collective-permute-start(bf16[4,512]{1,0:T(4,128)(2,1)S(1)} %halo_pass.1), channel_id=1, source_target_pairs={{0,4},{4,0},{1,5},{5,1},{2,6},{6,2},{3,7},{7,3},{8,12},{12,8},{9,1... | collective-permute-start | bytes 12296 | tf_op jit(solution)/shard_map/ppermute | solution.py:432
  9.0 1.2 %prepare.1 = (s32[32,512]{1,0:T(8,128)S(1)}, f32[512,128]{1,0:T(8,128)S(1)}, bf16[512,512]{1,0:T(8,128)(2,1)S(1)}, bf16[512,512]{1,0:T(8,128)(2,1)S(1)}) custom-call(s32[32,512]{1,0:T(8,128)} %bitcast.17, f32[512,128]{1,0:T(8,128)} %bitcast.15, bf16[512,512]{1,0:T(8,128)(2,1)} %weight_hbm.1), custom_call_target="tpu_custom_call" | custom-call | tf_op jit(solution)/shard_map/prepare/pallas_call | solution.py:421
  10.3 0.3 %collective-permute-done.3.refs_2_ = bf16[4,512]{1,0:T(4,128)(2,1)S(1)} collective-permute-done((bf16[4,512]{1,0:T(4,128)(2,1)S(1)}, bf16[4,512]{1,0:T(4,128)(2,1)S(1)}, u32[]{:S(2)}, u32[]{:S(2)}) %collective-permute-start.3) | collective-permute-done | bytes 4128 | tf_op jit(solution)/shard_map/ppermute | solution.py:435
  10.6 1.8 %forward_backward.1 = (bf16[256,128]{1,0:T(8,128)(2,1)S(1)}, bf16[256,512]{1,0:T(8,128)(2,1)S(1)}, bf16[128,512]{1,0:T(8,128)(2,1)S(1)}) custom-call(bf16[128,16]{1,0:T(8,128)(2,1)S(1)} %get-tuple-element.36.far_turned_ref, f32[128,512]{1,0:T(8,128)S(1)} %get-tuple-element.37.start_ref, s32[32,512]{1,0:T(8,128)S(1)} %get-tuple-element.38.candidates_ref, ...), custom_call_target="tpu_custom_call" | custom-call | tf_op jit(solution)/shard_map/forward_backward/pallas_call | solution.py:421
  12.4 0.8 %collective-permute-start.5 = (bf16[256,512]{1,0:T(8,128)(2,1)S(1)}, bf16[256,512]{1,0:T(8,128)(2,1)S(1)}, u32[]{:S(2)}, u32[]{:S(2)}) collective-permute-start(bf16[256,512]{1,0:T(8,128)(2,1)S(1)} %get-tuple-element.54), channel_id=1, source_target_pairs={{0,4},{4,0},{1,5},{5,1},{2,6},{6,2},{3,7},{7,3},{8,12},{12,8},{9,1... | collective-permute-start | bytes 786440 | tf_op jit(solution)/shard_map/ppermute | solution.py:432
  13.4 1.0 %collective-permute-done.5.arrived_ref = bf16[256,512]{1,0:T(8,128)(2,1)S(1)} collective-permute-done((bf16[256,512]{1,0:T(8,128)(2,1)S(1)}, bf16[256,512]{1,0:T(8,128)(2,1)S(1)}, u32[]{:S(2)}, u32[]{:S(2)}) %collective-permute-start.5) | collective-permute-done | bytes 262176 | tf_op jit(solution)/shard_map/ppermute | solution.py:432
  14.4 2.5 %collective-permute-start.6 = (bf16[256,128]{1,0:T(8,128)(2,1)S(1)}, bf16[256,128]{1,0:T(8,128)(2,1)S(1)}, u32[]{:S(2)}, u32[]{:S(2)}) collective-permute-start(bf16[256,128]{1,0:T(8,128)(2,1)S(1)} %get-tuple-element.56), channel_id=1, source_target_pairs={{0,3},{1,2},{2,1},{3,0},{4,7},{5,6},{6,5},{7,4},{8,11},{9,10},{10,... | collective-permute-start | bytes 196616 | tf_op jit(solution)/shard_map/ppermute | solution.py:449
  17.0 0.5 %collective-permute-start.7 = (bf16[256,128]{1,0:T(8,128)(2,1)S(1)}, bf16[256,128]{1,0:T(8,128)(2,1)S(1)}, u32[]{:S(2)}, u32[]{:S(2)}) collective-permute-start(bf16[256,128]{1,0:T(8,128)(2,1)S(1)} %get-tuple-element.57), channel_id=1, source_target_pairs={{0,2},{1,3},{2,0},{3,1},{4,6},{5,7},{6,4},{7,5},{8,10},{9,11},{10,... | collective-permute-start | bytes 196616 | tf_op jit(solution)/shard_map/ppermute | solution.py:449
  17.5 0.5 %collective-permute-start.8 = (bf16[256,128]{1,0:T(8,128)(2,1)S(1)}, bf16[256,128]{1,0:T(8,128)(2,1)S(1)}, u32[]{:S(2)}, u32[]{:S(2)}) collective-permute-start(bf16[256,128]{1,0:T(8,128)(2,1)S(1)} %get-tuple-element.58), channel_id=1, source_target_pairs={{0,1},{1,0},{2,3},{3,2},{4,5},{5,4},{6,7},{7,6},{8,9},{9,8},{10,11... | collective-permute-start | bytes 196616 | tf_op jit(solution)/shard_map/ppermute | solution.py:449
  18.0 0.5 %spread.1 = (f32[128,512]{1,0:T(8,128)S(1)}, f32[8,512]{1,0:T(8,128)S(1)}, f32[8,512]{1,0:T(8,128)S(1)}) custom-call(bf16[128,512]{1,0:T(8,128)(2,1)S(1)} %get-tuple-element.47.d_pre_ref, bf16[512,512]{1,0:T(8,128)(2,1)S(1)} %get-tuple-element.40.weight_ref, bf16[128,128]{1,0:T(8,128)(2,1)S(1)} %get-tuple-element.48.own_ref, ...), custom_call_target="tpu_custom_call" | custom-call | tf_op jit(solution)/shard_map/spread/pallas_call | solution.py:421
  18.6 1.2 %collective-permute-done.4.refs_5_.arrived_ref = f32[8,512]{1,0:T(8,128)S(1)} collective-permute-done((f32[8,512]{1,0:T(8,128)S(1)}, f32[8,512]{1,0:T(8,128)S(1)}, u32[]{:S(2)}, u32[]{:S(2)}) %collective-permute-start.4) | collective-permute-done | bytes 16416 | tf_op jit(solution)/shard_map/ppermute | solution.py:432
  19.8 1.4 %collective-permute-done.7.refs_2_ = bf16[256,128]{1,0:T(8,128)(2,1)S(1)} collective-permute-done((bf16[256,128]{1,0:T(8,128)(2,1)S(1)}, bf16[256,128]{1,0:T(8,128)(2,1)S(1)}, u32[]{:S(2)}, u32[]{:S(2)}) %collective-permute-start.7) | collective-permute-done | bytes 65568 | tf_op jit(solution)/shard_map/ppermute | solution.py:449
  21.2 0.5 %collective-permute-done.8.refs_3_ = bf16[256,128]{1,0:T(8,128)(2,1)S(1)} collective-permute-done((bf16[256,128]{1,0:T(8,128)(2,1)S(1)}, bf16[256,128]{1,0:T(8,128)(2,1)S(1)}, u32[]{:S(2)}, u32[]{:S(2)}) %collective-permute-start.8) | collective-permute-done | bytes 65568 | tf_op jit(solution)/shard_map/ppermute | solution.py:449
  21.8 0.3 %collective-permute-start.9 = (bf16[160,128]{1,0:T(8,128)(2,1)S(1)}, bf16[160,128]{1,0:T(8,128)(2,1)S(1)}, u32[]{:S(2)}, u32[]{:S(2)}) collective-permute-start(bf16[160,128]{1,0:T(8,128)(2,1)S(1)} %get-tuple-element.60), channel_id=1, source_target_pairs={{0,8},{4,28},{8,0},{12,20},{16,24},{20,12},{24,16},{28,4},{1,9},{5... | collective-permute-start | bytes 122888 | tf_op jit(solution)/shard_map/ppermute | solution.py:439
  22.1 3.2 %collective-permute-start.11 = (bf16[80,128]{1,0:T(8,128)(2,1)S(1)}, bf16[80,128]{1,0:T(8,128)(2,1)S(1)}, u32[]{:S(2)}, u32[]{:S(2)}) collective-permute-start(bf16[80,128]{1,0:T(8,128)(2,1)S(1)} %get-tuple-element.61), channel_id=1, source_target_pairs={{0,16},{8,24},{16,0},{24,8},{1,17},{9,25},{17,1},{25,9},{2,18},{10... | collective-permute-start | bytes 61448 | tf_op jit(solution)/shard_map/ppermute | solution.py:435
  25.3 0.7 %collective-permute-done.9.refs_0_ = bf16[160,128]{1,0:T(8,128)(2,1)S(1)} collective-permute-done((bf16[160,128]{1,0:T(8,128)(2,1)S(1)}, bf16[160,128]{1,0:T(8,128)(2,1)S(1)}, u32[]{:S(2)}, u32[]{:S(2)}) %collective-permute-start.9) | collective-permute-done | bytes 40992 | tf_op jit(solution)/shard_map/ppermute | solution.py:439
  26.2 0.9 %collective-permute-done.11.refs_2_ = bf16[80,128]{1,0:T(8,128)(2,1)S(1)} collective-permute-done((bf16[80,128]{1,0:T(8,128)(2,1)S(1)}, bf16[80,128]{1,0:T(8,128)(2,1)S(1)}, u32[]{:S(2)}, u32[]{:S(2)}) %collective-permute-start.11) | collective-permute-done | bytes 20512 | tf_op jit(solution)/shard_map/ppermute | solution.py:435
  27.3 0.9 %final.1 = (bf16[128,512]{1,0:T(8,128)(2,1)}, f32[64,128]{1,0:T(8,128)}) custom-call(f32[128,512]{1,0:T(8,128)S(1)} %get-tuple-element.49.local_ref, bf16[16,128]{1,0:T(8,128)(2,1)S(1)} %get-tuple-element.50.onehot_ref, f32[8,512]{1,0:T(8,128)S(1)} %get-tuple-element.51.refs_4_.kept_ref, f32[8,512]{1,0:T(8,128)S(1)} %collective-permute-done.4.refs_5_.arrived_ref, ...), custom_call_target="tpu_custom_call" | custom-call | tf_op jit(solution)/shard_map/final/pallas_call | solution.py:421
  (12 shorter events, 0.8 us)
Async XLA Ops:
  1.7 1.4 %collective-permute-start = (f32[8,512]{1,0:T(8,128)S(1)}, f32[8,512]{1,0:T(8,128)S(1)}, u32[]{:S(2)}, u32[]{:S(2)}) collective-permute-start(f32[8,512]{1,0:T(8,128)S(1)} %get-tuple-element.43), channel_id=1, source_target_pairs={{0,4},{4,0},{1,5},{5,1},{2,6},{6,2},{3,7},{7,3},{8,12},{12,8},{9,1... | collective-permute-start | bytes 49160 | tf_op jit(solution)/shard_map/ppermute | solution.py:432
  3.1 5.6 %collective-permute-start.1 = (bf16[8,512]{1,0:T(8,128)(2,1)S(1)}, bf16[8,512]{1,0:T(8,128)(2,1)S(1)}, u32[]{:S(2)}, u32[]{:S(2)}) collective-permute-start(bf16[8,512]{1,0:T(8,128)(2,1)S(1)} %get-tuple-element.45), channel_id=1, source_target_pairs={{0,8},{4,28},{8,0},{12,20},{16,24},{20,12},{24,16},{28,4},{1,9},{5... | collective-permute-start | bytes 24584 | tf_op jit(solution)/shard_map/ppermute | solution.py:439
  6.1 4.5 %collective-permute-start.3 = (bf16[4,512]{1,0:T(4,128)(2,1)S(1)}, bf16[4,512]{1,0:T(4,128)(2,1)S(1)}, u32[]{:S(2)}, u32[]{:S(2)}) collective-permute-start(bf16[4,512]{1,0:T(4,128)(2,1)S(1)} %get-tuple-element.46), channel_id=1, source_target_pairs={{0,16},{8,24},{16,0},{24,8},{1,17},{9,25},{17,1},{25,9},{2,18},{10... | collective-permute-start | bytes 12296 | tf_op jit(solution)/shard_map/ppermute | solution.py:435
  8.7 1.9 %collective-permute-start.2 = (bf16[4,512]{1,0:T(4,128)(2,1)S(1)}, bf16[4,512]{1,0:T(4,128)(2,1)S(1)}, u32[]{:S(2)}, u32[]{:S(2)}) collective-permute-start(bf16[4,512]{1,0:T(4,128)(2,1)S(1)} %halo_pass.1), channel_id=1, source_target_pairs={{0,4},{4,0},{1,5},{5,1},{2,6},{6,2},{3,7},{7,3},{8,12},{12,8},{9,1... | collective-permute-start | bytes 12296 | tf_op jit(solution)/shard_map/ppermute | solution.py:432
  12.4 1.9 %collective-permute-start.5 = (bf16[256,512]{1,0:T(8,128)(2,1)S(1)}, bf16[256,512]{1,0:T(8,128)(2,1)S(1)}, u32[]{:S(2)}, u32[]{:S(2)}) collective-permute-start(bf16[256,512]{1,0:T(8,128)(2,1)S(1)} %get-tuple-element.54), channel_id=1, source_target_pairs={{0,4},{4,0},{1,5},{5,1},{2,6},{6,2},{3,7},{7,3},{8,12},{12,8},{9,1... | collective-permute-start | bytes 786440 | tf_op jit(solution)/shard_map/ppermute | solution.py:432
  14.4 5.3 %collective-permute-start.6 = (bf16[256,128]{1,0:T(8,128)(2,1)S(1)}, bf16[256,128]{1,0:T(8,128)(2,1)S(1)}, u32[]{:S(2)}, u32[]{:S(2)}) collective-permute-start(bf16[256,128]{1,0:T(8,128)(2,1)S(1)} %get-tuple-element.56), channel_id=1, source_target_pairs={{0,3},{1,2},{2,1},{3,0},{4,7},{5,6},{6,5},{7,4},{8,11},{9,10},{10,... | collective-permute-start | bytes 196616 | tf_op jit(solution)/shard_map/ppermute | solution.py:449
  17.0 4.3 %collective-permute-start.7 = (bf16[256,128]{1,0:T(8,128)(2,1)S(1)}, bf16[256,128]{1,0:T(8,128)(2,1)S(1)}, u32[]{:S(2)}, u32[]{:S(2)}) collective-permute-start(bf16[256,128]{1,0:T(8,128)(2,1)S(1)} %get-tuple-element.57), channel_id=1, source_target_pairs={{0,2},{1,3},{2,0},{3,1},{4,6},{5,7},{6,4},{7,5},{8,10},{9,11},{10,... | collective-permute-start | bytes 196616 | tf_op jit(solution)/shard_map/ppermute | solution.py:449
  17.5 4.3 %collective-permute-start.8 = (bf16[256,128]{1,0:T(8,128)(2,1)S(1)}, bf16[256,128]{1,0:T(8,128)(2,1)S(1)}, u32[]{:S(2)}, u32[]{:S(2)}) collective-permute-start(bf16[256,128]{1,0:T(8,128)(2,1)S(1)} %get-tuple-element.58), channel_id=1, source_target_pairs={{0,1},{1,0},{2,3},{3,2},{4,5},{5,4},{6,7},{7,6},{8,9},{9,8},{10,11... | collective-permute-start | bytes 196616 | tf_op jit(solution)/shard_map/ppermute | solution.py:449
  18.5 1.2 %collective-permute-start.4 = (f32[8,512]{1,0:T(8,128)S(1)}, f32[8,512]{1,0:T(8,128)S(1)}, u32[]{:S(2)}, u32[]{:S(2)}) collective-permute-start(f32[8,512]{1,0:T(8,128)S(1)} %get-tuple-element.52), channel_id=1, source_target_pairs={{0,4},{4,0},{1,5},{5,1},{2,6},{6,2},{3,7},{7,3},{8,12},{12,8},{9,1... | collective-permute-start | bytes 49160 | tf_op jit(solution)/shard_map/ppermute | solution.py:432
  21.8 4.3 %collective-permute-start.9 = (bf16[160,128]{1,0:T(8,128)(2,1)S(1)}, bf16[160,128]{1,0:T(8,128)(2,1)S(1)}, u32[]{:S(2)}, u32[]{:S(2)}) collective-permute-start(bf16[160,128]{1,0:T(8,128)(2,1)S(1)} %get-tuple-element.60), channel_id=1, source_target_pairs={{0,8},{4,28},{8,0},{12,20},{16,24},{20,12},{24,16},{28,4},{1,9},{5... | collective-permute-start | bytes 122888 | tf_op jit(solution)/shard_map/ppermute | solution.py:439
  22.1 5.0 %collective-permute-start.11 = (bf16[80,128]{1,0:T(8,128)(2,1)S(1)}, bf16[80,128]{1,0:T(8,128)(2,1)S(1)}, u32[]{:S(2)}, u32[]{:S(2)}) collective-permute-start(bf16[80,128]{1,0:T(8,128)(2,1)S(1)} %get-tuple-element.61), channel_id=1, source_target_pairs={{0,16},{8,24},{16,0},{24,8},{1,17},{9,25},{17,1},{25,9},{2,18},{10... | collective-permute-start | bytes 61448 | tf_op jit(solution)/shard_map/ppermute | solution.py:435
  26.1 1.3 %collective-permute-start.10 = (bf16[80,128]{1,0:T(8,128)(2,1)S(1)}, bf16[80,128]{1,0:T(8,128)(2,1)S(1)}, u32[]{:S(2)}, u32[]{:S(2)}) collective-permute-start(bf16[80,128]{1,0:T(8,128)(2,1)S(1)} %pass_sums.1), channel_id=1, source_target_pairs={{0,4},{4,0},{1,5},{5,1},{2,6},{6,2},{3,7},{7,3},{8,12},{12,8},{9,1... | collective-permute-start | bytes 61448 | tf_op jit(solution)/shard_map/ppermute | solution.py:432
